TPU v7x, 128 devices: a whole 4x4x4 slice. The times are simulated.
128 devices in a mesh: loop: 8 (over x_lo, z), rep: 16 (over x_hi, y, core).
Axes of the slice: x: 4 (x_hi: 2, x_lo: 2; x = x_hi * 2 + x_lo), y: 4, z: 4, core: 2. Of those that a mesh axis runs over, the one named last changes fastest.
Arguments:
- features: bfloat16 [16, 4096, 2048], P('rep', 'loop'), may hold values from -8 to 8
- weight: bfloat16 [2048, 512], P(('loop', 'rep')), may hold values from -0.125 to 0.125
- pair_ids: int32 [16, 4096], P('rep', 'loop'), may hold values from 0 to 2047, as said below
- dup_ids: int32 [16, 4096], P('rep', 'loop'), may hold values from 0 to 682, as said below
Outputs:
- image_loss: float32 [16, 4096], P('rep', 'loop')
- feature_grad: bfloat16 [16, 4096, 2048], P('rep', 'loop')
- weight_grad: float32 [2048, 512], P(('loop', 'rep'))
Inputs may be any that keep to these rules, and one draw needn't show every extreme that they name: `pair_ids`: within one replica every value is held by exactly two images. Images with equal pair_ids have equal dup_ids; within one replica a value is shared by at most three pairs.
All inputs are finite; a program needn't handle non-finite values.
Results may differ from a plain program's by a relative error of at most 0.013.
Values may be sent and summed in bfloat16 or wider, within the bound.
A program may use at most 64 MiB of HBM per device.

v0:
```python
import math

import jax
import jax.numpy as jnp
from jax import lax
from jax.sharding import PartitionSpec as P

scale_logits = 20.0
norm_eps = 1e-06


def pair_masks(row_dups, row_pairs, row_first, col_dups, col_pairs):
    row_index = row_first + jnp.arange(row_dups.shape[0], dtype=jnp.int32)
    col_index = jnp.arange(col_dups.shape[0], dtype=jnp.int32)
    distinct = row_index[:, None] != col_index[None, :]
    partner = jnp.logical_and(row_pairs[:, None] == col_pairs[None, :], distinct)
    allowed = jnp.logical_and(
        distinct, jnp.logical_or(row_dups[:, None] != col_dups[None, :], partner)
    )
    return (allowed.astype(jnp.float32), partner.astype(jnp.float32))


def pair_scores(left_embed, right_embed):
    return scale_logits * jnp.dot(left_embed, right_embed.T, preferred_element_type=jnp.float32)


def body(features, weight, pair_ids, dup_ids):
    image_feats = features[0]
    pair_labels = pair_ids[0]
    dup_labels = dup_ids[0]
    row_count = image_feats.shape[0]
    own_first = lax.axis_index("loop") * row_count
    full_weight = lax.all_gather(weight, ("loop", "rep"), axis=0, tiled=True)
    projected = jnp.dot(image_feats, full_weight, preferred_element_type=jnp.float32)
    inverse_norm = lax.rsqrt(jnp.sum(projected * projected, axis=1, keepdims=True) + norm_eps)
    normed = projected * inverse_norm
    embedding = normed.astype(jnp.bfloat16)
    col_embed = lax.all_gather(embedding, "loop", axis=0, tiled=True)
    col_dups = lax.all_gather(dup_labels, "loop", axis=0, tiled=True)
    col_pairs = lax.all_gather(pair_labels, "loop", axis=0, tiled=True)
    scores = pair_scores(embedding, col_embed)
    allowed, partner = pair_masks(dup_labels, pair_labels, own_first, col_dups, col_pairs)
    exp_total = jnp.sum(allowed * jnp.exp(scores - scale_logits), axis=1)
    positive = jnp.sum(partner * scores, axis=1)
    exp_total, positive = (exp_total, positive)
    log_total = jnp.log(exp_total) + scale_logits
    whole_norm = lax.all_gather(log_total, "loop", axis=0, tiled=True)
    col_embed = lax.all_gather(embedding, "loop", axis=0, tiled=True)
    col_dups = lax.all_gather(dup_labels, "loop", axis=0, tiled=True)
    col_pairs = lax.all_gather(pair_labels, "loop", axis=0, tiled=True)
    scores = pair_scores(embedding, col_embed)
    allowed, partner = pair_masks(dup_labels, pair_labels, own_first, col_dups, col_pairs)
    row_weight = (allowed * jnp.exp(scores - log_total[:, None]) - partner).astype(jnp.bfloat16)
    col_weight = (allowed * jnp.exp(scores - whole_norm[None, :]) - partner).astype(jnp.bfloat16)
    running = jnp.dot(row_weight, col_embed, preferred_element_type=jnp.float32)
    grad_sum = running + jnp.dot(col_weight, col_embed, preferred_element_type=jnp.float32)
    image_loss = log_total - positive
    grad_embed = scale_logits * grad_sum
    grad_pre = (
        inverse_norm * (grad_embed - normed * jnp.sum(normed * grad_embed, axis=1, keepdims=True))
    ).astype(jnp.bfloat16)
    feature_grad = jnp.dot(grad_pre, full_weight.T, preferred_element_type=jnp.float32).astype(
        jnp.bfloat16
    )
    total_count = row_count * lax.axis_size("loop") * lax.axis_size("rep")
    summed = lax.psum_scatter(
        lax.dot_general(
            image_feats, grad_pre, (((0,), (0,)), ((), ())), preferred_element_type=jnp.float32
        ),
        ("loop", "rep"),
        scatter_dimension=0,
        tiled=True,
    )
    weight_grad = summed / math.sqrt(total_count)
    return (image_loss[None, :], feature_grad[None], weight_grad)


def solution(mesh):
    return jax.shard_map(
        body,
        mesh=mesh,
        in_specs=(
            P("rep", "loop", None),
            P(("loop", "rep"), None),
            P("rep", "loop"),
            P("rep", "loop"),
        ),
        out_specs=(P("rep", "loop"), P("rep", "loop", None), P(("loop", "rep"), None)),
        check_vma=False,
    )
```

profile of v0, /device:TPU:0, one launch (start us, length us, event | category | flops | bytes accessed | tf_op | source)
XLA Modules:
  0.0 968.7 jit_solution(9479523133286328542)
XLA Ops:
  7.2 0.0 copy-start
  7.2 0.0 all-gather.6.cloned.1.call-start
  7.2 0.7 all-gather.6.cloned.1.call-update
  7.9 0.0 copy-start.3
  7.9 0.0 copy-start.4
  7.9 0.0 all-gather.8.cloned.1.call-start
  8.0 198.7 %all-gather.6.cloned.1.call-done = bf16[2048,512]{1,0:T(8,128)(2,1)} async-done(((bf16[16,512]{1,0:T(8,128)(2,1)}), bf16[2048,512]{1,0:T(8,128)(2,1)}) %all-gather.6.cloned.1.call-update) | async-done | bytes 2097168 | tf_op jit(solution)/shard_map/all_gather | solution.py:33
  206.7 0.0 copy-done
  206.7 2.9 multiply_reduce_fusion.1
  209.6 0.9 multiply_convert_fusion.1
  210.5 0.0 all-gather.8.cloned.1.call-update
  210.5 0.0 reduce-scatter.4.cloned.1.call-start
  210.6 0.0 copy-done.3
  210.6 23.7 %all-gather.1 = s32[1,4096]{1,0:T(1,128)S(1)} all-gather(s32[1,512]{1,0:T(1,128)S(1)} %copy-done.3), channel_id=3, replica_groups=mesh['loop'=8,'rep'=16] {'loop'}, dimensions={1}, use_global_device_ids=true | all-gather | bytes 18432 | tf_op jit(solution)/shard_map/all_gather | solution.py:40
  234.3 23.7 %all-gather = s32[1,4096]{1,0:T(1,128)S(1)} all-gather(s32[1,512]{1,0:T(1,128)S(1)} %copy-done.4), channel_id=2, replica_groups=mesh['loop'=8,'rep'=16] {'loop'}, dimensions={1}, use_global_device_ids=true | all-gather | bytes 18432 | tf_op jit(solution)/shard_map/all_gather | solution.py:39
  258.0 4.4 all-gather.8.cloned.1.call-done
  262.3 9.7 select_reduce_fusion.1
  272.0 0.6 log_add_fusion
  272.6 23.8 %all-gather.2 = f32[8,1,512]{2,1,0:T(1,128)S(1)} all-gather(f32[1,1,512]{2,1,0:T(1,128)S(1)} %bitcast.34), channel_id=1, replica_groups=mesh['loop'=8,'rep'=16] {'loop'}, dimensions={0}, use_global_device_ids=true | all-gather | bytes 18432 | tf_op jit(solution)/shard_map/all_gather | solution.py:47
  296.4 5.9 fusion.4
  302.4 6.1 multiply_reduce_fusion
  308.4 0.3 multiply_convert_fusion
  308.7 0.0 copy-start.1
  308.7 0.8 copy-done.1
  309.5 3.4 convolution_bitcast_fusion
  312.9 5.3 copy.9
  318.3 0.0 reduce-scatter.4.cloned.1.call-update
  318.3 1.0 copy-done.2
  319.3 4.2 fusion.14
  323.6 637.0 %reduce-scatter.4.cloned.1.call-done = f32[16,512]{1,0:T(8,128)} async-done(((f32[2048,512]{1,0:T(8,128)}), f32[16,512]{1,0:T(8,128)}) %reduce-scatter.4.cloned.1.call-update) | async-done | bytes 32784
  960.5 0.9 copy.10
  961.5 0.7 copy.8
  (7 shorter events, 0.0 us)
Async XLA Ops:
  7.2 199.5 %copy-start = (bf16[1,512,2048]{2,1,0:T(8,128)(2,1)S(1)}, bf16[1,512,2048]{2,1,0:T(8,128)(2,1)}, u32[]{:S(2)}) copy-start(bf16[1,512,2048]{2,1,0:T(8,128)(2,1)} %param.4) | copy-start | bytes 6291460
  7.2 199.5 %all-gather.6.cloned.1.call-start = ((), (), s32[]{:S(2)}) async-start(), calls=%async_computation.1 | async-start | bytes 2113536 | tf_op jit(solution)/shard_map/all_gather | solution.py:33
  7.9 202.7 %copy-start.3 = (s32[1,512]{1,0:T(1,128)S(1)}, s32[1,512]{1,0:T(1,128)}, u32[]{:S(2)}) copy-start(s32[1,512]{1,0:T(1,128)} %param.6) | copy-start | bytes 6148
  7.9 226.4 %copy-start.4 = (s32[1,512]{1,0:T(1,128)S(1)}, s32[1,512]{1,0:T(1,128)}, u32[]{:S(2)}) copy-start(s32[1,512]{1,0:T(1,128)} %param.7) | copy-start | bytes 6148
  7.9 254.4 %all-gather.8.cloned.1.call-start = ((), (), s32[]{:S(2)}) async-start(), calls=%async_computation.2 | async-start | bytes 4718592 | tf_op jit(solution)/shard_map/all_gather | solution.py:38
  210.5 750.0 %reduce-scatter.4.cloned.1.call-start = ((), (), s32[]{:S(2)}) async-start(), calls=%async_computation.3 | async-start | bytes 4227072
  262.3 34.1 %copy-start.5 = (bf16[4096,512]{0,1:T(8,128)(2,1)S(1)}, bf16[4096,512]{0,1:T(8,128)(2,1)}, u32[]{:S(2)}) copy-start(bf16[4096,512]{0,1:T(8,128)(2,1)} %all-gather.8.cloned.1.call-done) | copy-start | bytes 12582916
  308.7 0.8 copy-start.1
  318.3 1.0 copy-start.2
Sparse Core Ops, SparseCore 0:
  9.7 196.9 all-gather.5
  210.7 51.5 all-gather.7
  318.4 642.0 reduce-scatter.3
where the time goes:
time: 969 us
  waiting for transfers between devices  841 us (87%)
  blocking collectives  71.2 us (7%)
  matrix products  32.2 us (3%)
  between operations  13.8 us (1%)
    unnamed x4, waiting for transfers between devices  638 us
    all_gather x1, waiting for transfers between devices, body(): full_weight = lax.all_gather(weight, ('loop', 'rep'), axis=0, tiled=True)  199 us
    all_gather x1, blocking collectives, body(): whole_norm = lax.all_gather(log_total, 'loop', axis=0, tiled=True)  23.8 us
    all_gather x1, blocking collectives, body(): col_pairs = lax.all_gather(pair_labels, 'loop', axis=0, tiled=True)  23.7 us
    all_gather x1, blocking collectives, body(): col_dups = lax.all_gather(dup_labels, 'loop', axis=0, tiled=True)  23.7 us
  transfers between devices with their start and end apart: 3, of which 3 were waited for; matrix products, arithmetic and copies ran while one was open for 0% of the time, Pallas kernels for 0%

commit v1 on v0

v1 whole, which is shorter than its diff:
```python
import jax
import jax.numpy as jnp
from jax import lax
from jax.experimental import pallas as pl
from jax.experimental.pallas import tpu as pltpu
from jax.sharding import PartitionSpec as P

MESH = pl.DeviceIdType.MESH
scale_logits = 20.0
norm_eps = 1e-06
ROWS = 512
FEAT = 2048
EMB = 512
HALF = 256
BF16 = jnp.bfloat16
F32 = jnp.float32

ORDER = (
    (1, 0, 0),
    (1, 0, 1),
    (0, 3, 0),
    (0, 1, 1),
    (0, 3, 1),
    (0, 1, 0),
    (1, 3, 0),
    (1, 1, 1),
    (1, 3, 1),
    (1, 1, 0),
    (0, 2, 0),
    (0, 2, 1),
    (1, 2, 0),
    (1, 2, 1),
)


def device_at(x, y, z, core):
    return (lax.rem(x, 2) * 4 + z, lax.div(x, 2) * 8 + y * 2 + core)


def remote(src, dst, send_sem, recv_sem, device):
    return pltpu.make_async_remote_copy(
        src_ref=src,
        dst_ref=dst,
        send_sem=send_sem,
        recv_sem=recv_sem,
        device_id=device,
        device_id_type=MESH,
    )


def pick(step, column):
    value = jnp.int32(0)
    for index, entry in enumerate(ORDER):
        if entry[column]:
            value = jnp.where(step == index, entry[column], value)
    return value


def to_row(column):
    return jnp.broadcast_to(column, (ROWS, 128)).T[0:8, :]


def to_column(rows):
    return rows.T


def kernel(
    feat_hbm,
    weight_ref,
    pair_ref,
    dup_ref,
    loss_ref,
    fgrad_hbm,
    wgrad_ref,
    feat,
    featp,
    wpart,
    wfull,
    normed,
    inverse,
    home_emb,
    emb,
    labels,
    label_home,
    row_labels,
    dots,
    quot,
    acc,
    pos,
    norms,
    grad,
    grad_out,
    grad_in,
    aux_out,
    aux_in,
    pre,
    fgrad,
    sib_out,
    sib_in,
    first_out,
    first_in,
    first_sum,
    second_out,
    second_in,
    third_out,
    third_in,
    feat_sem,
    fgrad_sem,
    wx_send,
    wx_recv,
    ws_send,
    ws_recv,
    wf_send,
    wf_recv,
    wc_send,
    wc_recv,
    lab_send,
    lab_recv,
    labx_send,
    labx_recv,
    swap_send,
    swap_recv,
    ring_send,
    sib_send,
    emb_recv,
    norm_send,
    norm_recv,
    back_send,
    back_recv,
    rc_send,
    rc_recv,
    rf_send,
    rf_recv,
    rs_send,
    rs_recv,
    rx_send,
    rx_recv,
):
    loop, rep = lax.axis_index("loop"), lax.axis_index("rep")
    x_lo, z = lax.div(loop, 4), lax.rem(loop, 4)
    x_hi, y, core = lax.div(rep, 8), lax.rem(lax.div(rep, 2), 4), lax.rem(rep, 2)
    x = x_hi * 2 + x_lo
    other = 1 - core
    first = z * other + y * core
    second = y * other + z * core
    stays = core == x_lo
    slot = core * 4 + z

    def around(value, step):
        return lax.rem(value + step, 4)

    def x_peer(step):
        return device_at(around(x, step), y, z, core)

    def first_peer(step):
        return device_at(
            x, around(y, step * core), around(z, step * other), core
        )

    def second_peer(step):
        return device_at(
            x, around(y, step * other), around(z, step * core), core
        )

    def z_peer(step, which):
        return device_at(x, y, around(z, step), which)

    sibling = device_at(x, y, z, other)
    partner = device_at(x_hi * 2 + 1 - x_lo, y, z, other)

    load = pltpu.make_async_copy(feat_hbm, feat, feat_sem)
    load.start()

    barrier = pltpu.get_barrier_semaphore()
    everyone = [sibling, partner]
    for step in (1, 2, 3):
        everyone += [x_peer(step), first_peer(step), second_peer(step), z_peer(step, other)]
    for device in everyone:
        pl.semaphore_signal(barrier, inc=1, device_id=device, device_id_type=MESH)

    wpart[core, first, second, x] = weight_ref[...]
    label_home[...] = jnp.zeros((8, ROWS), jnp.int32)
    label_home[0:1, :] = pair_ref[...]
    label_home[1:2, :] = dup_ref[...]
    pl.semaphore_wait(barrier, len(everyone))

    wx = [
        remote(
            wpart.at[core, first, second, x],
            wpart.at[core, first, second, x],
            wx_send.at[step - 1],
            wx_recv.at[step - 1],
            x_peer(step),
        )
        for step in (1, 2, 3)
    ]
    for copy in wx:
        copy.start()

    lab_swap = remote(label_home, labels.at[other * 4 + z], labx_send.at[0], labx_recv.at[0], partner)
    lab_swap_in = remote(label_home, labels.at[slot], labx_send.at[0], labx_recv.at[0], partner)

    @pl.when(jnp.logical_not(stays))
    def _():
        lab_swap.start()

    @pl.when(stays)
    def _():
        labels[slot] = label_home[...]

    load.wait()

    def transpose_slab(slab, carry):
        slab_xlo, slab_z, slab_xhi = lax.div(slab, 8), lax.rem(lax.div(slab, 2), 4), lax.rem(slab, 2)
        slab_x = slab_xhi * 2 + slab_xlo
        turned = feat[:, pl.ds(pl.multiple_of(slab * 128, 128), 128)].T
        for at_y in range(4):
            zero = pl.multiple_of((at_y * 4 + slab_x) * 16, 16)
            featp[0, slab_z, pl.ds(zero, 16), :] = turned[at_y * 32 : at_y * 32 + 16]
            one = pl.multiple_of((slab_z * 4 + slab_x) * 16, 16)
            featp[1, at_y, pl.ds(one, 16), :] = turned[at_y * 32 + 16 : at_y * 32 + 32]
        return carry

    for step in (1, 2, 3):
        source = around(x, 4 - step)
        remote(
            wpart.at[core, first, second, source],
            wpart.at[core, first, second, source],
            wx_send.at[step - 1],
            wx_recv.at[step - 1],
            x_peer(step),
        ).wait_recv()
    started = list(wx)
    for step in (1, 2, 3):
        copy = remote(
            wpart.at[core, first, second],
            wpart.at[core, first, second],
            ws_send.at[step - 1],
            ws_recv.at[step - 1],
            second_peer(step),
        )
        copy.start()
        started.append(copy)
    for piece in range(4):
        source = around(second, 4 - piece)
        if piece:
            remote(
                wpart.at[core, first, source],
                wpart.at[core, first, source],
                ws_send.at[piece - 1],
                ws_recv.at[piece - 1],
                second_peer(piece),
            ).wait_recv()
        for step in (1, 2, 3):
            copy = remote(
                wpart.at[core, first, source],
                wpart.at[core, first, source],
                wf_send.at[step - 1, piece],
                wf_recv.at[step - 1, piece],
                first_peer(step),
            )
            copy.start()
            started.append(copy)
    to_sibling = remote(
        wpart.at[core, first], wpart.at[core, first], wc_send.at[0], wc_recv.at[0], sibling
    )
    to_sibling.start()
    started.append(to_sibling)

    lax.fori_loop(0, 16, transpose_slab, 0)

    @pl.when(jnp.logical_not(stays))
    def _():
        lab_swap_in.wait_recv()

    lab_copies = []
    for index, (step, which) in enumerate(
        [(0, other)] + [(step, which) for step in (1, 2, 3) for which in (core, other)]
    ):
        copy = remote(
            labels.at[slot],
            labels.at[slot],
            lab_send.at[index],
            lab_recv.at[slot],
            z_peer(step, which),
        )
        copy.start()
        lab_copies.append(copy)
    row_labels[...] = to_column(labels[slot])

    for step in (1, 2, 3):
        source = around(first, 4 - step)
        for piece in range(4):
            at = around(second, 4 - piece)
            remote(
                wpart.at[core, source, at],
                wpart.at[core, source, at],
                wf_send.at[step - 1, piece],
                wf_recv.at[step - 1, piece],
                first_peer(step),
            ).wait_recv()
        copy = remote(
            wpart.at[core, source],
            wpart.at[core, source],
            wc_send.at[step],
            wc_recv.at[step],
            sibling,
        )
        copy.start()
        started.append(copy)
    sibling_first = second
    for step in range(4):
        source = around(sibling_first, 4 - step)
        remote(
            wpart.at[other, source],
            wpart.at[other, source],
            wc_send.at[step],
            wc_recv.at[step],
            sibling,
        ).wait_recv()

    def place_block(index, carry):
        at_first, at_second, at_x = lax.div(index, 16), lax.rem(lax.div(index, 4), 4), lax.rem(index, 4)
        base = lax.rem(at_x, 2) * 64 + lax.div(at_x, 2) * 8
        zero = (base + at_first * 16 + at_second * 2) * 16
        one = (base + at_second * 16 + at_first * 2 + 1) * 16
        wfull[pl.ds(pl.multiple_of(zero, 16), 16), :] = wpart[0, at_first, at_second, at_x]
        wfull[pl.ds(pl.multiple_of(one, 16), 16), :] = wpart[1, at_first, at_second, at_x]
        return carry

    lax.fori_loop(0, 64, place_block, 0)

    def project(index, carry):
        columns = pl.ds(pl.multiple_of(index * HALF, HALF), HALF)
        normed[:, columns] = jnp.dot(feat[...], wfull[:, columns], preferred_element_type=F32)
        return carry

    lax.fori_loop(0, 2, project, 0)

    def normalise(index, carry):
        rows = pl.ds(pl.multiple_of(index * 64, 64), 64)
        projected = normed[rows, :]
        scale = lax.rsqrt(jnp.sum(projected * projected, axis=1, keepdims=True) + norm_eps)
        unit = projected * scale
        normed[rows, :] = unit
        inverse[rows, :] = jnp.broadcast_to(scale, (64, 128))
        home_emb[rows, :] = unit.astype(BF16)
        return carry

    lax.fori_loop(0, 8, normalise, 0)

    def half(ref, at, which):
        return ref.at[at, pl.ds(pl.multiple_of(which * HALF, HALF), HALF)]

    swaps = [
        remote(
            home_emb.at[pl.ds(part * HALF, HALF)],
            emb.at[other * 4 + z, pl.ds(part * HALF, HALF)],
            swap_send.at[part],
            swap_recv.at[part],
            partner,
        )
        for part in range(2)
    ]

    @pl.when(jnp.logical_not(stays))
    def _():
        for copy in swaps:
            copy.start()

    @pl.when(stays)
    def _():
        emb[slot] = home_emb[...]

    acc[...] = jnp.zeros((ROWS, 128), F32)
    pos[...] = jnp.zeros((ROWS, 128), F32)

    def ring(at, which, step, sem):
        return remote(
            half(emb, at, which), half(emb, at, which), ring_send.at[sem], emb_recv.at[at, which], z_peer(step, core)
        )

    def beside(at, which, sem):
        return remote(
            half(emb, at, which), half(emb, at, which), sib_send.at[sem], emb_recv.at[at, which], sibling
        )

    for part in range(2):

        @pl.when(jnp.logical_not(stays))
        def _():
            remote(
                home_emb.at[pl.ds(part * HALF, HALF)],
                emb.at[slot, pl.ds(part * HALF, HALF)],
                swap_send.at[part],
                swap_recv.at[part],
                partner,
            ).wait_recv()

        ring(slot, part, 1, part).start()
        ring(slot, part, 3, 2 + part).start()
        beside(slot, part, part).start()

    for index in range(7):
        other_slot = lax.rem(slot + 1 + index, 8)
        remote(
            labels.at[other_slot],
            labels.at[other_slot],
            lab_send.at[index],
            lab_recv.at[other_slot],
            sibling,
        ).wait_recv()

    def take(at, which, own):
        piece = at * 2 + which
        dots[...] = lax.dot_general(
            emb[slot],
            emb[at, pl.ds(pl.multiple_of(which * HALF, HALF), HALF), :],
            (((1,), (1,)), ((), ())),
            preferred_element_type=F32,
        )
        columns = pl.ds(pl.multiple_of(which * HALF, HALF), HALF)
        col_pair = labels[at, 0:1, columns]
        col_dup = labels[at, 1:2, columns]

        def rows_of(index, carry):
            start = pl.multiple_of(index * 64, 64)
            rows = pl.ds(start, 64)
            row_pair = row_labels[rows, 0:1]
            row_dup = row_labels[rows, 1:2]
            scores = scale_logits * dots[rows, :]
            mate = row_pair == col_pair
            allowed = jnp.logical_or(row_dup != col_dup, mate)
            if own:
                row_index = start + lax.broadcasted_iota(jnp.int32, (64, HALF), 0)
                col_index = which * HALF + lax.broadcasted_iota(jnp.int32, (64, HALF), 1)
                distinct = row_index != col_index
                mate = jnp.logical_and(mate, distinct)
                allowed = jnp.logical_and(allowed, distinct)
            weight = jnp.where(allowed, jnp.exp(scores - scale_logits), 0.0)
            quot[piece, rows, :] = weight
            acc[rows, :] += weight[:, :128] + weight[:, 128:]
            matched = jnp.where(mate, scores, 0.0)
            pos[rows, :] += matched[:, :128] + matched[:, 128:]
            return carry

        lax.fori_loop(0, 8, rows_of, 0)

    def own_piece(part, carry):
        take(slot, part, True)
        return carry

    lax.fori_loop(0, 2, own_piece, 0)

    def next_piece(step, carry):
        which_ring = jnp.where(pick(step, 0) == 0, core, other)
        at = which_ring * 4 + around(z, pick(step, 1))
        which = pick(step, 2)
        ring(at, which, 1, 0).wait_recv()

        @pl.when(step == 2)
        def _():
            ring(at, which, 1, 4).start()
            beside(at, which, 2).start()

        @pl.when(step == 3)
        def _():
            ring(at, which, 3, 5).start()
            beside(at, which, 3).start()

        for index, count in ((4, 4), (5, 5), (10, 6), (11, 7)):

            @pl.when(step == index)
            def _():
                beside(at, which, count).start()

        take(at, which, False)
        return carry

    lax.fori_loop(0, len(ORDER), next_piece, 0)

    total = jnp.sum(acc[...], axis=1, keepdims=True)
    loss = jnp.log(total) + scale_logits - jnp.sum(pos[...], axis=1, keepdims=True)
    own_norm = 1.0 / total
    norms[slot] = to_row(own_norm)
    norm_copies = []
    for index, (step, which) in enumerate(
        [(0, other)] + [(step, which) for step in (1, 2, 3) for which in (core, other)]
    ):
        copy = remote(
            norms.at[slot], norms.at[slot], norm_send.at[index], norm_recv.at[slot], z_peer(step, which)
        )
        copy.start()
        norm_copies.append(copy)
    acc[...] = jnp.broadcast_to(own_norm, (ROWS, 128))
    pos[...] = jnp.broadcast_to(loss, (ROWS, 128))
    aux_out[...] = to_row(loss)
    for index in range(7):
        other_slot = lax.rem(slot + 1 + index, 8)
        remote(
            norms.at[other_slot],
            norms.at[other_slot],
            norm_send.at[index],
            norm_recv.at[other_slot],
            sibling,
        ).wait_recv()

    for part in range(2):
        rows = pl.ds(part * HALF, HALF)
        row_pair = row_labels[rows, 0:1]
        row_norm = acc[rows, 0:1]

        def add_slot(at, carry):
            for which in range(2):
                columns = pl.ds(which * HALF, HALF)
                mate = row_pair == labels[at, 0:1, columns]
                own = jnp.logical_and(
                    at == slot,
                    part * HALF + lax.broadcasted_iota(jnp.int32, (HALF, HALF), 0)
                    == which * HALF + lax.broadcasted_iota(jnp.int32, (HALF, HALF), 1),
                )
                mate = jnp.logical_and(mate, jnp.logical_not(own))
                weight = quot[at * 2 + which, rows, :] * (row_norm + norms[at, 0:1, columns])
                weight = weight - jnp.where(mate, 2.0, 0.0)
                term = jnp.dot(weight.astype(BF16), emb[at, columns, :], preferred_element_type=F32)
                grad[rows, :] += term
            return carry

        grad[rows, :] = jnp.zeros((HALF, EMB), F32)
        lax.fori_loop(0, 8, add_slot, 0)

        @pl.when(jnp.logical_not(stays))
        def _():
            unit = emb[slot, rows, :].astype(F32)
            whole = grad[rows, :]
            along = jnp.sum(unit * whole, axis=1, keepdims=True)
            grad_out[rows, :] = (whole - along * unit).astype(BF16)
            inner = jnp.broadcast_to(along, (HALF, 128)).T[0:1, :]
            aux_out[1:2, part * HALF : (part + 1) * HALF] = inner
            remote(
                grad_out.at[rows], grad_in.at[rows], back_send.at[part], back_recv.at[part], partner
            ).start()

    @pl.when(jnp.logical_not(stays))
    def _():
        remote(aux_out, aux_in, back_send.at[2], back_recv.at[2], partner).start()
        remote(aux_out, aux_in, back_send.at[2], back_recv.at[2], partner).wait_recv()
        columns_of = to_column(aux_in[...])
        loss_ref[...] = aux_in[0:1, :]
        for part in range(2):
            rows = pl.ds(part * HALF, HALF)
            remote(
                grad_out.at[rows], grad_in.at[rows], back_send.at[part], back_recv.at[part], partner
            ).wait_recv()
            along = columns_of[part * HALF : (part + 1) * HALF, 1:2]
            grad[rows, :] = grad_in[rows, :].astype(F32) + along * home_emb[rows, :].astype(F32)

    @pl.when(stays)
    def _():
        loss_ref[...] = aux_out[0:1, :]

    def finish(index, carry):
        rows = pl.ds(pl.multiple_of(index * 64, 64), 64)
        unit = normed[rows, :]
        whole = scale_logits * grad[rows, :]
        along = jnp.sum(unit * whole, axis=1, keepdims=True)
        pre[rows, :] = (inverse[rows, 0:1] * (whole - unit * along)).astype(BF16)
        return carry

    lax.fori_loop(0, 8, finish, 0)

    def term_of(which, at):
        return jnp.dot(featp[which, at], pre[...], preferred_element_type=F32)

    reduce_copies = []
    for step in range(4):
        at = around(sibling_first, step + 1 if step < 3 else 0)
        sib_out[step] = term_of(other, at).astype(BF16)
        copy = remote(sib_out.at[step], sib_in.at[step], rc_send.at[step], rc_recv.at[step], sibling)
        copy.start()
        reduce_copies.append(copy)
    for step in range(4):
        at = around(first, step + 1 if step < 3 else 0)
        own = term_of(core, at)
        remote(sib_out.at[step], sib_in.at[step], rc_send.at[step], rc_recv.at[step], sibling).wait_recv()
        own = own + sib_in[step].astype(F32)
        if step < 3:
            first_out[step] = own.astype(BF16)
            copy = remote(
                first_out.at[step], first_in.at[step], rf_send.at[step], rf_recv.at[step], first_peer(step + 1)
            )
            copy.start()
            reduce_copies.append(copy)
        else:
            first_sum[...] = own

    def feature_part(index, carry):
        columns = pl.ds(pl.multiple_of(index * 512, 512), 512)
        fgrad[:, columns] = lax.dot_general(
            pre[...], wfull[columns, :], (((1,), (1,)), ((), ())), preferred_element_type=F32
        ).astype(BF16)
        return carry

    lax.fori_loop(0, 4, feature_part, 0)
    store = pltpu.make_async_copy(fgrad, fgrad_hbm, fgrad_sem)
    store.start()

    for step in range(3):
        remote(
            first_out.at[step], first_in.at[step], rf_send.at[step], rf_recv.at[step], first_peer(step + 1)
        ).wait_recv()

    def first_rows(at):
        rows = pl.ds(pl.multiple_of(at * 64, 64), 64)
        value = first_sum[rows, :]
        for step in range(3):
            value = value + first_in[step, rows, :].astype(F32)
        return value

    for step in range(3):
        second_out[step] = first_rows(around(second, step + 1)).astype(BF16)
        copy = remote(
            second_out.at[step], second_in.at[step], rs_send.at[step], rs_recv.at[step], second_peer(step + 1)
        )
        copy.start()
        reduce_copies.append(copy)
    second_sum = first_rows(second)
    for step in range(3):
        remote(
            second_out.at[step], second_in.at[step], rs_send.at[step], rs_recv.at[step], second_peer(step + 1)
        ).wait_recv()
        second_sum = second_sum + second_in[step].astype(F32)
    first_sum[0:64, :] = second_sum
    for step in range(3):
        rows = pl.ds(pl.multiple_of(around(x, step + 1) * 16, 16), 16)
        third_out[step] = first_sum[rows, :].astype(BF16)
        copy = remote(
            third_out.at[step], third_in.at[step], rx_send.at[step], rx_recv.at[step], x_peer(step + 1)
        )
        copy.start()
        reduce_copies.append(copy)
    value = first_sum[pl.ds(pl.multiple_of(x * 16, 16), 16), :]
    for step in range(3):
        remote(
            third_out.at[step], third_in.at[step], rx_send.at[step], rx_recv.at[step], x_peer(step + 1)
        ).wait_recv()
        value = value + third_in[step].astype(F32)
    wgrad_ref[...] = value * (1.0 / 256.0)

    for copy in started + lab_copies + norm_copies + reduce_copies:
        copy.wait_send()
    for index in range(6):
        ring(slot, 0, 1, index).wait_send()
    for index in range(8):
        beside(slot, 0, index).wait_send()

    @pl.when(jnp.logical_not(stays))
    def _():
        lab_swap.wait_send()
        for copy in swaps:
            copy.wait_send()
        for part in range(2):
            rows = pl.ds(part * HALF, HALF)
            remote(
                grad_out.at[rows], grad_in.at[rows], back_send.at[part], back_recv.at[part], partner
            ).wait_send()
        remote(aux_out, aux_in, back_send.at[2], back_recv.at[2], partner).wait_send()

    store.wait()


def body(features, weight, pair_ids, dup_ids):
    dma = pltpu.SemaphoreType.DMA
    vmem = pltpu.VMEM
    loss, feature_grad, weight_grad = pl.pallas_call(
        kernel,
        out_shape=(
            jax.ShapeDtypeStruct((1, ROWS), F32),
            jax.ShapeDtypeStruct((ROWS, FEAT), BF16),
            jax.ShapeDtypeStruct((16, EMB), F32),
        ),
        in_specs=[
            pl.BlockSpec(memory_space=pl.ANY),
            pl.BlockSpec(memory_space=vmem),
            pl.BlockSpec(memory_space=vmem),
            pl.BlockSpec(memory_space=vmem),
        ],
        out_specs=(
            pl.BlockSpec(memory_space=vmem),
            pl.BlockSpec(memory_space=pl.ANY),
            pl.BlockSpec(memory_space=vmem),
        ),
        scratch_shapes=[
            vmem((ROWS, FEAT), BF16),
            vmem((2, 4, 256, EMB), BF16),
            vmem((2, 4, 4, 4, 16, EMB), BF16),
            vmem((FEAT, EMB), BF16),
            vmem((ROWS, EMB), F32),
            vmem((ROWS, 128), F32),
            vmem((ROWS, EMB), BF16),
            vmem((8, ROWS, EMB), BF16),
            vmem((8, 8, ROWS), jnp.int32),
            vmem((8, ROWS), jnp.int32),
            vmem((ROWS, 8), jnp.int32),
            vmem((ROWS, HALF), F32),
            vmem((16, ROWS, HALF), F32),
            vmem((ROWS, 128), F32),
            vmem((ROWS, 128), F32),
            vmem((8, 8, ROWS), F32),
            vmem((ROWS, EMB), F32),
            vmem((ROWS, EMB), BF16),
            vmem((ROWS, EMB), BF16),
            vmem((8, ROWS), F32),
            vmem((8, ROWS), F32),
            vmem((ROWS, EMB), BF16),
            vmem((ROWS, FEAT), BF16),
            vmem((4, 256, EMB), BF16),
            vmem((4, 256, EMB), BF16),
            vmem((3, 256, EMB), BF16),
            vmem((3, 256, EMB), BF16),
            vmem((256, EMB), F32),
            vmem((3, 64, EMB), BF16),
            vmem((3, 64, EMB), BF16),
            vmem((3, 16, EMB), BF16),
            vmem((3, 16, EMB), BF16),
            dma,
            dma,
            dma((3,)),
            dma((3,)),
            dma((3,)),
            dma((3,)),
            dma((3, 4)),
            dma((3, 4)),
            dma((4,)),
            dma((4,)),
            dma((7,)),
            dma((8,)),
            dma((1,)),
            dma((1,)),
            dma((2,)),
            dma((2,)),
            dma((6,)),
            dma((8,)),
            dma((8, 2)),
            dma((7,)),
            dma((8,)),
            dma((3,)),
            dma((3,)),
            dma((4,)),
            dma((4,)),
            dma((3,)),
            dma((3,)),
            dma((3,)),
            dma((3,)),
            dma((3,)),
            dma((3,)),
        ],
        compiler_params=pltpu.CompilerParams(
            collective_id=0, has_side_effects=True, vmem_limit_bytes=56 << 20
        ),
        cost_estimate=pl.CostEstimate(
            flops=7_500_000_000, bytes_accessed=8 << 20, transcendentals=2 << 20
        ),
        name="infonce",
    )(features[0], weight, pair_ids, dup_ids)
    return loss, feature_grad[None], weight_grad


def solution(mesh):
    return jax.shard_map(
        body,
        mesh=mesh,
        in_specs=(
            P("rep", "loop", None),
            P(("loop", "rep"), None),
            P("rep", "loop"),
            P("rep", "loop"),
        ),
        out_specs=(P("rep", "loop"), P("rep", "loop", None), P(("loop", "rep"), None)),
        check_vma=False,
    )
```

time: 969 us -> 99.1 us (0.10)
  waiting for transfers between devices: 841 us -> 0 us
  Pallas kernels: 0 us -> 93.2 us
  blocking collectives: 71.2 us -> 0 us
  matrix products: 32.2 us -> 0 us
  between operations: 13.8 us -> 0.64 us
    unnamed x4 -> x0, waiting for transfers between devices: 638 us -> none
    all_gather x2 -> x0, waiting for transfers between devices: 203 us -> none  [the longest x1 199 us: body(): full_weight = lax.all_gather(weight, ('loop', 'rep'), axis=0, tiled=True)]
    pallas_call x0 -> x1, Pallas kernels: none -> 93.2 us  [body(): pl.pallas_call(kernel, out_shape=(jax.ShapeDtypeStruct((1, ROWS), F32), j...]
    all_gather x3 -> x0, blocking collectives: 71.2 us -> none  [the longest x1 23.8 us: body(): whole_norm = lax.all_gather(log_total, 'loop', axis=0, tiled=True)]
    dot_general x6 -> x0, matrix products: 32.2 us -> none  [the longest x1 9.67 us: pair_scores(): jnp.dot(left_embed, right_embed.T, preferred_element_type=jnp.float32)]
  transfers between devices with their start and end apart: 3 -> 0, of which waited for: 3 -> 0; matrix products, arithmetic and copies ran while one was open for 0% -> 0% of each run, Pallas kernels for 0% -> 0%
where the time goes in v1:
time: 99.1 us; the launch traced here: 98.9 us
  Pallas kernels  93.2 us (94%)
  local copies, waits for them, and re-layouts  5.03 us (5%)
    pallas_call x1, Pallas kernels, body(): pl.pallas_call(kernel, out_shape=(jax.ShapeDtypeStruct((1, ROWS), F32), j...  93.2 us
    unnamed x5, local copies, waits for them, and re-layouts  5.03 us

profile of v1, /device:TPU:0, one launch (start us, length us, event | category | flops | bytes accessed | tf_op | source)
XLA Modules:
  0.0 98.9 jit_solution(14501138128783306477)
XLA Ops:
  0.6 93.2 %infonce.1 = (f32[1,512]{1,0:T(1,128)}, bf16[512,2048]{1,0:T(8,128)(2,1)}, f32[16,512]{1,0:T(8,128)}) custom-call(bf16[512,2048]{1,0:T(8,128)(2,1)} %bitcast.3, bf16[16,512]{1,0:T(8,128)(2,1)} %weight_ref.1, s32[1,512]{1,0:T(1,128)} %pair_ref.1, s32[1,512]{1,0:T(1,128)} %dup_ref.1), custom_call_target="tpu_custom_call" | custom-call | flops 7500000256 | bytes 8388608 | tf_op jit(solution)/shard_map/infonce/pallas_call | solution.py:675
  93.8 1.2 %copy.10 = f32[1,512]{1,0:T(1,128)} copy(f32[1,512]{1,0:T(1,128)} %get-tuple-element.12) | data formatting | bytes 4096
  95.1 0.0 copy-start
  95.1 3.2 %copy.11 = bf16[1,512,2048]{2,1,0:T(8,128)(2,1)} copy(bf16[1,512,2048]{2,1,0:T(8,128)(2,1)} %bitcast.2) | data formatting | bytes 4194304
  98.2 0.0 copy-done
  98.2 0.6 copy.12
Async XLA Ops:
  95.1 3.2 %copy-start = (f32[16,512]{1,0:T(8,128)S(1)}, f32[16,512]{1,0:T(8,128)}, u32[]{:S(2)}) copy-start(f32[16,512]{1,0:T(8,128)} %get-tuple-element.14) | copy-start | bytes 98308

commit v2 on v1

v2 whole, which is shorter than its diff:
```python
import jax
import jax.numpy as jnp
from jax import lax
from jax.experimental import pallas as pl
from jax.experimental.pallas import tpu as pltpu
from jax.sharding import PartitionSpec as P

MESH = pl.DeviceIdType.MESH
scale_logits = 20.0
norm_eps = 1e-06
ROWS = 512
FEAT = 2048
EMB = 512
HALF = 256
SLOPE = 28.853900817779268
BF16 = jnp.bfloat16
F32 = jnp.float32

ORDER = (
    (0, 3, 0),
    (0, 1, 0),
    (1, 0, 0),
    (0, 1, 1),
    (0, 3, 1),
    (1, 0, 1),
    (1, 3, 0),
    (1, 1, 0),
    (1, 1, 1),
    (1, 3, 1),
    (0, 2, 0),
    (0, 2, 1),
    (1, 2, 0),
    (1, 2, 1),
)
STEPS = (0, 1, 3, 2)
FAR_FIRST = (2, 1, 3, 0)
PLANE = (10, 6, 14, 9, 11, 2, 8, 5, 7, 13, 15, 1, 3, 4, 12)


def device_at(x, y, z, core):
    return (lax.rem(x, 2) * 4 + z, lax.div(x, 2) * 8 + y * 2 + core)


def remote(src, dst, send_sem, recv_sem, device):
    return pltpu.make_async_remote_copy(
        src_ref=src,
        dst_ref=dst,
        send_sem=send_sem,
        recv_sem=recv_sem,
        device_id=device,
        device_id_type=MESH,
    )


def pick(step, column):
    value = jnp.int32(0)
    for index, entry in enumerate(ORDER):
        if entry[column]:
            value = jnp.where(step == index, entry[column], value)
    return value


def to_column(rows):
    return rows.T


def kernel(
    feat_hbm,
    weight_ref,
    pair_ref,
    dup_ref,
    loss_ref,
    fgrad_hbm,
    wgrad_ref,
    feat,
    featp,
    wpart,
    wfull,
    normed,
    inverse,
    home_emb,
    emb,
    labels,
    label_home,
    row_pairs,
    row_dups,
    weights,
    dots,
    quot,
    acc,
    pos,
    norms,
    grad,
    grad_out,
    grad_in,
    aux_out,
    aux_in,
    pre,
    fgrad,
    sib_out,
    sib_in,
    own_term,
    first_out,
    first_in,
    first_sum,
    plane_out,
    plane_in,
    feat_sem,
    fgrad_sem,
    wp_send,
    wp_recv,
    wf_send,
    wf_recv,
    wc_send,
    wc_recv,
    lab_send,
    lab_recv,
    labx_send,
    labx_recv,
    swap_send,
    swap_recv,
    ring_send,
    sib_send,
    emb_recv,
    norm_send,
    norm_recv,
    back_send,
    back_recv,
    rc_send,
    rc_recv,
    rf_send,
    rf_recv,
    rp_send,
    rp_recv,
):
    loop, rep = lax.axis_index("loop"), lax.axis_index("rep")
    x_lo, z = lax.div(loop, 4), lax.rem(loop, 4)
    x_hi, y, core = lax.div(rep, 8), lax.rem(lax.div(rep, 2), 4), lax.rem(rep, 2)
    x = x_hi * 2 + x_lo
    other = 1 - core
    first = z * other + y * core
    second = y * other + z * core
    stays = core == x_lo
    slot = core * 4 + z

    def around(value, step):
        return lax.rem(value + step, 4)

    def plane_peer(index):
        step = index // 4
        return device_at(
            around(x, index % 4), around(y, step * other), around(z, step * core), core
        )

    def first_peer(step):
        return device_at(
            x, around(y, step * core), around(z, step * other), core
        )

    def z_peer(step, which):
        return device_at(x, y, around(z, step), which)

    sibling = device_at(x, y, z, other)
    partner = device_at(x_hi * 2 + 1 - x_lo, y, z, other)

    load = pltpu.make_async_copy(feat_hbm, feat, feat_sem)
    load.start()

    barrier = pltpu.get_barrier_semaphore()
    everyone = [sibling, partner] + [plane_peer(index) for index in range(1, 16)]
    for step in (1, 2, 3):
        everyone += [first_peer(step), z_peer(step, other)]
    for device in everyone:
        pl.semaphore_signal(barrier, inc=1, device_id=device, device_id_type=MESH)

    wpart[core, first, second, x] = weight_ref[...]
    label_home[...] = jnp.zeros((8, ROWS), jnp.int32)
    label_home[0:1, :] = pair_ref[...]
    label_home[1:2, :] = dup_ref[...]
    pl.semaphore_wait(barrier, len(everyone))

    started = []
    for index in PLANE:
        copy = remote(
            wpart.at[core, first, second, x],
            wpart.at[core, first, second, x],
            wp_send.at[index - 1],
            wp_recv.at[index - 1],
            plane_peer(index),
        )
        copy.start()
        started.append(copy)

    lab_swap = remote(label_home, labels.at[other * 4 + z], labx_send.at[0], labx_recv.at[0], partner)
    lab_swap_in = remote(label_home, labels.at[slot], labx_send.at[0], labx_recv.at[0], partner)

    @pl.when(jnp.logical_not(stays))
    def _():
        lab_swap.start()

    @pl.when(stays)
    def _():
        labels[slot] = label_home[...]

    load.wait()

    def transpose_slab(slab, carry):
        slab_xlo, slab_z, slab_xhi = lax.div(slab, 8), lax.rem(lax.div(slab, 2), 4), lax.rem(slab, 2)
        slab_x = slab_xhi * 2 + slab_xlo
        turned = feat[:, pl.ds(pl.multiple_of(slab * 128, 128), 128)].T
        for at_y in range(4):
            zero = pl.multiple_of((at_y * 4 + slab_x) * 16, 16)
            featp[0, slab_z, pl.ds(zero, 16), :] = turned[at_y * 32 : at_y * 32 + 16]
            one = pl.multiple_of((slab_z * 4 + slab_x) * 16, 16)
            featp[1, at_y, pl.ds(one, 16), :] = turned[at_y * 32 + 16 : at_y * 32 + 32]
        return carry

    def give(source_first, source_second, at):
        copy = remote(
            wpart.at[core, source_first, source_second],
            wpart.at[core, source_first, source_second],
            wc_send.at[at],
            wc_recv.at[at],
            sibling,
        )
        copy.start()
        started.append(copy)

    for piece in STEPS:
        source = around(second, 4 - piece)
        for index in range(piece * 4, piece * 4 + 4):
            if index:
                block = wpart.at[core, first, source, around(x, 4 - index % 4)]
                remote(
                    block, block, wp_send.at[index - 1], wp_recv.at[index - 1], plane_peer(index)
                ).wait_recv()
        for step in (2, 1, 3):
            copy = remote(
                wpart.at[core, first, source],
                wpart.at[core, first, source],
                wf_send.at[step - 1, piece],
                wf_recv.at[step - 1, piece],
                first_peer(step),
            )
            copy.start()
            started.append(copy)
        give(first, source, piece)

    lax.fori_loop(0, 16, transpose_slab, 0)

    @pl.when(jnp.logical_not(stays))
    def _():
        lab_swap_in.wait_recv()

    lab_copies = []
    for index, (step, which) in enumerate(
        [(0, other)] + [(step, which) for step in (1, 2, 3) for which in (core, other)]
    ):
        copy = remote(
            labels.at[slot],
            labels.at[slot],
            lab_send.at[index],
            lab_recv.at[slot],
            z_peer(step, which),
        )
        copy.start()
        lab_copies.append(copy)
    turned_labels = to_column(labels[slot])
    row_pairs[...] = jnp.broadcast_to(turned_labels[:, 0:1], (ROWS, 128))
    row_dups[...] = jnp.broadcast_to(turned_labels[:, 1:2], (ROWS, 128))

    for piece in STEPS:
        at = around(second, 4 - piece)
        for step in (1, 3, 2):
            source = around(first, 4 - step)
            remote(
                wpart.at[core, source, at],
                wpart.at[core, source, at],
                wf_send.at[step - 1, piece],
                wf_recv.at[step - 1, piece],
                first_peer(step),
            ).wait_recv()
            give(source, at, step * 4 + piece)
    for piece in STEPS:
        for step in range(4):
            block = wpart.at[other, around(second, 4 - step), around(first, 4 - piece)]
            at = step * 4 + piece
            remote(block, block, wc_send.at[at], wc_recv.at[at], sibling).wait_recv()

    def place_block(index, carry):
        at_first, at_second, at_x = lax.div(index, 16), lax.rem(lax.div(index, 4), 4), lax.rem(index, 4)
        base = lax.rem(at_x, 2) * 64 + lax.div(at_x, 2) * 8
        zero = (base + at_first * 16 + at_second * 2) * 16
        one = (base + at_second * 16 + at_first * 2 + 1) * 16
        wfull[pl.ds(pl.multiple_of(zero, 16), 16), :] = wpart[0, at_first, at_second, at_x]
        wfull[pl.ds(pl.multiple_of(one, 16), 16), :] = wpart[1, at_first, at_second, at_x]
        return carry

    lax.fori_loop(0, 64, place_block, 0, unroll=8)

    def half(ref, at, which):
        return ref.at[at, pl.ds(pl.multiple_of(which * HALF, HALF), HALF)]

    def ring(at, which, step, sem):
        return remote(
            half(emb, at, which), half(emb, at, which), ring_send.at[sem], emb_recv.at[at, which], z_peer(step, core)
        )

    def beside(at, which, sem):
        return remote(
            half(emb, at, which), half(emb, at, which), sib_send.at[sem], emb_recv.at[at, which], sibling
        )

    def send_own(part):
        ring(slot, part, 1, part).start()
        ring(slot, part, 3, 2 + part).start()
        beside(slot, part, part).start()

    swaps = [
        remote(
            home_emb.at[pl.ds(part * HALF, HALF)],
            emb.at[other * 4 + z, pl.ds(part * HALF, HALF)],
            swap_send.at[part],
            swap_recv.at[part],
            partner,
        )
        for part in range(2)
    ]
    for part in range(2):
        half_rows = pl.ds(part * HALF, HALF)
        normed[half_rows, :] = jnp.dot(feat[half_rows, :], wfull[...], preferred_element_type=F32)
        for start in range(part * HALF, part * HALF + HALF, 64):
            rows = pl.ds(start, 64)
            projected = normed[rows, :]
            scale = lax.rsqrt(jnp.sum(projected * projected, axis=1, keepdims=True) + norm_eps)
            unit = projected * scale
            normed[rows, :] = unit
            inverse[rows, :] = jnp.broadcast_to(scale, (64, 128))
            home_emb[rows, :] = unit.astype(BF16)

        @pl.when(jnp.logical_not(stays))
        def _():
            swaps[part].start()

        @pl.when(stays)
        def _():
            emb[slot, half_rows, :] = home_emb[half_rows, :]
            send_own(part)

    acc[...] = jnp.zeros((ROWS, 128), F32)
    pos[...] = jnp.zeros((ROWS, 128), F32)

    @pl.when(jnp.logical_not(stays))
    def _():
        for part in range(2):
            remote(
                home_emb.at[pl.ds(part * HALF, HALF)],
                emb.at[slot, pl.ds(part * HALF, HALF)],
                swap_send.at[part],
                swap_recv.at[part],
                partner,
            ).wait_recv()
            send_own(part)

    for index in range(7):
        other_slot = lax.rem(slot + 1 + index, 8)
        remote(
            labels.at[other_slot],
            labels.at[other_slot],
            lab_send.at[index],
            lab_recv.at[other_slot],
            sibling,
        ).wait_recv()

    def take(at, which, own):
        piece = at * 2 + which
        columns = pl.ds(pl.multiple_of(which * HALF, HALF), HALF)
        dots[...] = lax.dot_general(
            emb[slot], emb[at, columns, :], (((1,), (1,)), ((), ())), preferred_element_type=F32
        )
        for part in range(2):
            lanes = pl.ds(pl.multiple_of(which * HALF + part * 128, 128), 128)
            col_pair = labels[at, 0:1, lanes]
            col_dup = labels[at, 1:2, lanes]
            for start in range(0, ROWS, 64):
                rows = pl.ds(start, 64)
                power = dots[rows, part * 128 : (part + 1) * 128] * SLOPE - SLOPE
                value = jnp.exp2(power)
                mate = row_pairs[rows, :] == col_pair
                if own:
                    row_index = start + lax.broadcasted_iota(jnp.int32, (64, 128), 0)
                    col_index = which * HALF + part * 128 + lax.broadcasted_iota(jnp.int32, (64, 128), 1)
                    mate = jnp.logical_and(mate, row_index != col_index)
                apart = jnp.where(row_dups[rows, :] != col_dup, value, 0.0)
                paired = jnp.where(mate, value, 0.0)
                quot[piece, rows, part * 128 : (part + 1) * 128] = apart - paired
                acc[rows, :] += apart
                pos[rows, :] += paired

    def own_piece(part, carry):
        take(slot, part, True)
        return carry

    lax.fori_loop(0, 2, own_piece, 0)

    def next_piece(step, carry):
        which_ring = jnp.where(pick(step, 0) == 0, core, other)
        at = which_ring * 4 + around(z, pick(step, 1))
        which = pick(step, 2)
        ring(at, which, 1, 0).wait_recv()

        @pl.when(step == 0)
        def _():
            ring(at, which, 1, 4).start()
            beside(at, which, 2).start()

        @pl.when(step == 3)
        def _():
            ring(at, which, 3, 5).start()
            beside(at, which, 3).start()

        for index, count in ((1, 4), (4, 5), (10, 6), (11, 7)):

            @pl.when(step == index)
            def _():
                beside(at, which, count).start()

        take(at, which, False)
        return carry

    lax.fori_loop(0, len(ORDER), next_piece, 0)

    paired_row = jnp.sum(pos[...].T, axis=0, keepdims=True)
    total_row = jnp.sum(acc[...].T, axis=0, keepdims=True) + paired_row
    norms[slot] = jnp.broadcast_to(1.0 / total_row, (8, ROWS))
    norm_copies = []
    for index, (step, which) in enumerate(
        [(0, other)] + [(step, which) for step in (1, 2, 3) for which in (core, other)]
    ):
        copy = remote(
            norms.at[slot], norms.at[slot], norm_send.at[index], norm_recv.at[slot], z_peer(step, which)
        )
        copy.start()
        norm_copies.append(copy)
    aux_out[...] = jnp.broadcast_to(jnp.log(total_row) - jnp.log(paired_row), (8, ROWS))
    total = jnp.sum(acc[...] + pos[...], axis=1, keepdims=True)
    acc[...] = jnp.broadcast_to(1.0 / total, (ROWS, 128))

    def wait_norm(at):
        remote(norms.at[at], norms.at[at], norm_send.at[0], norm_recv.at[at], sibling).wait_recv()

    for part in range(2):
        rows = pl.ds(part * HALF, HALF)

        def add_slots(step, carry):
            at_z = around(z, jnp.where(step < 2, step, 5 - step))
            pair = (core * 4 + at_z, other * 4 + at_z)
            if part == 0:

                @pl.when(step > 0)
                def _():
                    wait_norm(pair[0])

                wait_norm(pair[1])
            for index, at in enumerate(pair):
                for lane in range(0, ROWS, 128):
                    norm = norms[at, 0:1, lane : lane + 128]
                    for start in range(0, HALF, 64):
                        take_rows = pl.ds(part * HALF + start, 64)
                        value = quot[at * 2 + lane // HALF, take_rows, lane % HALF : lane % HALF + 128]
                        weight = jnp.abs(value) * (acc[take_rows, :] + norm) - jnp.where(value < 0.0, 2.0, 0.0)
                        weights[start : start + 64, index * ROWS + lane : index * ROWS + lane + 128] = weight.astype(BF16)
            grad[rows, :] += jnp.dot(
                weights[:, :ROWS], emb[pair[0]], preferred_element_type=F32
            ) + jnp.dot(weights[:, ROWS:], emb[pair[1]], preferred_element_type=F32)
            return carry

        grad[rows, :] = jnp.zeros((HALF, EMB), F32)
        lax.fori_loop(0, 4, add_slots, 0)

        @pl.when(jnp.logical_not(stays))
        def _():
            unit = emb[slot, rows, :].astype(F32)
            whole = grad[rows, :]
            along = jnp.sum(unit * whole, axis=1, keepdims=True)
            grad_out[rows, :] = (whole - along * unit).astype(BF16)
            inner = jnp.broadcast_to(along, (HALF, 128)).T[0:1, :]
            aux_out[1:2, part * HALF : (part + 1) * HALF] = inner
            remote(
                grad_out.at[rows], grad_in.at[rows], back_send.at[part], back_recv.at[part], partner
            ).start()

    @pl.when(jnp.logical_not(stays))
    def _():
        remote(aux_out, aux_in, back_send.at[2], back_recv.at[2], partner).start()
        remote(aux_out, aux_in, back_send.at[2], back_recv.at[2], partner).wait_recv()
        columns_of = to_column(aux_in[...])
        loss_ref[...] = aux_in[0:1, :]
        for part in range(2):
            rows = pl.ds(part * HALF, HALF)
            remote(
                grad_out.at[rows], grad_in.at[rows], back_send.at[part], back_recv.at[part], partner
            ).wait_recv()
            along = columns_of[part * HALF : (part + 1) * HALF, 1:2]
            grad[rows, :] = grad_in[rows, :].astype(F32) + along * home_emb[rows, :].astype(F32)

    @pl.when(stays)
    def _():
        loss_ref[...] = aux_out[0:1, :]

    def finish(index, carry):
        rows = pl.ds(pl.multiple_of(index * 64, 64), 64)
        unit = normed[rows, :]
        whole = scale_logits * grad[rows, :]
        along = jnp.sum(unit * whole, axis=1, keepdims=True)
        pre[rows, :] = (inverse[rows, 0:1] * (whole - unit * along)).astype(BF16)
        return carry

    lax.fori_loop(0, 8, finish, 0, unroll=True)

    def term_of(which, at):
        return jnp.dot(featp[which, at], pre[...], preferred_element_type=F32)

    reduce_copies = []
    for at in range(4):
        term = term_of(other, at).astype(BF16)
        for group in range(4):
            sib_out[group, at] = term[group * 64 : group * 64 + 64]
    for index, offset in enumerate(FAR_FIRST):
        group = around(first, offset)
        copy = remote(sib_out.at[group], sib_in.at[group], rc_send.at[index], rc_recv.at[index], sibling)
        copy.start()
        reduce_copies.append(copy)
    for at in range(4):
        own_term[at] = term_of(core, at)
    for index, offset in enumerate(FAR_FIRST):
        group = around(second, offset)
        remote(
            sib_out.at[group], sib_in.at[group], rc_send.at[index], rc_recv.at[index], sibling
        ).wait_recv()
        rows = pl.ds(pl.multiple_of(group * 64, 64), 64)
        for count, step in enumerate(FAR_FIRST):
            at = around(first, step)
            value = own_term[at, rows, :] + sib_in[group, at].astype(F32)
            if step:
                first_out[index, count] = value.astype(BF16)
                copy = remote(
                    first_out.at[index, count],
                    first_in.at[index, count],
                    rf_send.at[index * 3 + count],
                    rf_recv.at[index * 3 + count],
                    first_peer(step),
                )
                copy.start()
                reduce_copies.append(copy)
            else:
                first_sum[index] = value

    def feature_part(index, carry):
        columns = pl.ds(pl.multiple_of(index * 512, 512), 512)
        fgrad[:, columns] = lax.dot_general(
            pre[...], wfull[columns, :], (((1,), (1,)), ((), ())), preferred_element_type=F32
        ).astype(BF16)
        return carry

    lax.fori_loop(0, 4, feature_part, 0)
    store = pltpu.make_async_copy(fgrad, fgrad_hbm, fgrad_sem)
    store.start()

    for index, offset in enumerate(FAR_FIRST):
        whole = first_sum[index]
        for count in (1, 2, 0):
            remote(
                first_out.at[index, count],
                first_in.at[index, count],
                rf_send.at[index * 3 + count],
                rf_recv.at[index * 3 + count],
                first_peer(1),
            ).wait_recv()
            whole = whole + first_in[index, count].astype(F32)
        plane_out[index] = whole.astype(BF16)
        for step in FAR_FIRST:
            target = offset * 4 + step
            if target:
                copy = remote(
                    plane_out.at[index, pl.ds(pl.multiple_of(around(x, step) * 16, 16), 16)],
                    plane_in.at[target - 1],
                    rp_send.at[target - 1],
                    rp_recv.at[target - 1],
                    plane_peer(target),
                )
                copy.start()
                reduce_copies.append(copy)
        if offset == 0:
            first_sum[index] = whole
    value = first_sum[3, pl.ds(pl.multiple_of(x * 16, 16), 16), :]
    for offset in FAR_FIRST:
        for step in (1, 3, 2, 0):
            target = offset * 4 + step
            if target:
                remote(
                    plane_out.at[0, pl.ds(0, 16)],
                    plane_in.at[target - 1],
                    rp_send.at[target - 1],
                    rp_recv.at[target - 1],
                    plane_peer(target),
                ).wait_recv()
                value = value + plane_in[target - 1].astype(F32)
    wgrad_ref[...] = value * (1.0 / 256.0)

    for copy in started + lab_copies + norm_copies + reduce_copies:
        copy.wait_send()
    for index in range(6):
        ring(slot, 0, 1, index).wait_send()
    for index in range(8):
        beside(slot, 0, index).wait_send()

    @pl.when(jnp.logical_not(stays))
    def _():
        lab_swap.wait_send()
        for copy in swaps:
            copy.wait_send()
        for part in range(2):
            rows = pl.ds(part * HALF, HALF)
            remote(
                grad_out.at[rows], grad_in.at[rows], back_send.at[part], back_recv.at[part], partner
            ).wait_send()
        remote(aux_out, aux_in, back_send.at[2], back_recv.at[2], partner).wait_send()

    store.wait()


def deliver(loss_in, fgrad_in, wgrad_in, loss_out, fgrad_out, wgrad_out, loss, fgrad, wgrad, load_sem, store_sem):
    parts = [
        (fgrad_in.at[pl.ds(at, 128)], fgrad.at[pl.ds(at, 128)], fgrad_out.at[pl.ds(at, 128)])
        for at in range(0, ROWS, 128)
    ]
    parts += [(loss_in, loss, loss_out), (wgrad_in, wgrad, wgrad_out)]
    loads = [
        pltpu.make_async_copy(source, held, load_sem.at[index]) for index, (source, held, _) in enumerate(parts)
    ]
    stores = [
        pltpu.make_async_copy(held, target, store_sem.at[index]) for index, (_, held, target) in enumerate(parts)
    ]
    for copy in loads:
        copy.start()
    for load, store in zip(loads, stores):
        load.wait()
        store.start()
    for store in stores:
        store.wait()


def body(features, weight, pair_ids, dup_ids):
    dma = pltpu.SemaphoreType.DMA
    vmem = pltpu.VMEM
    loss, feature_grad, weight_grad = pl.pallas_call(
        kernel,
        out_shape=(
            jax.ShapeDtypeStruct((1, ROWS), F32),
            jax.ShapeDtypeStruct((ROWS, FEAT), BF16),
            jax.ShapeDtypeStruct((16, EMB), F32),
        ),
        in_specs=[
            pl.BlockSpec(memory_space=pl.ANY),
            pl.BlockSpec(memory_space=vmem),
            pl.BlockSpec(memory_space=vmem),
            pl.BlockSpec(memory_space=vmem),
        ],
        out_specs=(
            pl.BlockSpec(memory_space=vmem),
            pl.BlockSpec(memory_space=pl.ANY),
            pl.BlockSpec(memory_space=vmem),
        ),
        scratch_shapes=[
            vmem((ROWS, FEAT), BF16),
            vmem((2, 4, 256, EMB), BF16),
            vmem((2, 4, 4, 4, 16, EMB), BF16),
            vmem((FEAT, EMB), BF16),
            vmem((ROWS, EMB), F32),
            vmem((ROWS, 128), F32),
            vmem((ROWS, EMB), BF16),
            vmem((8, ROWS, EMB), BF16),
            vmem((8, 8, ROWS), jnp.int32),
            vmem((8, ROWS), jnp.int32),
            vmem((ROWS, 128), jnp.int32),
            vmem((ROWS, 128), jnp.int32),
            vmem((HALF, 2 * ROWS), BF16),
            vmem((ROWS, HALF), F32),
            vmem((16, ROWS, HALF), F32),
            vmem((ROWS, 128), F32),
            vmem((ROWS, 128), F32),
            vmem((8, 8, ROWS), F32),
            vmem((ROWS, EMB), F32),
            vmem((ROWS, EMB), BF16),
            vmem((ROWS, EMB), BF16),
            vmem((8, ROWS), F32),
            vmem((8, ROWS), F32),
            vmem((ROWS, EMB), BF16),
            vmem((ROWS, FEAT), BF16),
            vmem((4, 4, 64, EMB), BF16),
            vmem((4, 4, 64, EMB), BF16),
            vmem((4, 256, EMB), F32),
            vmem((4, 3, 64, EMB), BF16),
            vmem((4, 3, 64, EMB), BF16),
            vmem((4, 64, EMB), F32),
            vmem((4, 64, EMB), BF16),
            vmem((15, 16, EMB), BF16),
            dma,
            dma,
            dma((15,)),
            dma((15,)),
            dma((3, 4)),
            dma((3, 4)),
            dma((16,)),
            dma((16,)),
            dma((7,)),
            dma((8,)),
            dma((1,)),
            dma((1,)),
            dma((2,)),
            dma((2,)),
            dma((6,)),
            dma((8,)),
            dma((8, 2)),
            dma((7,)),
            dma((8,)),
            dma((3,)),
            dma((3,)),
            dma((4,)),
            dma((4,)),
            dma((12,)),
            dma((12,)),
            dma((15,)),
            dma((15,)),
        ],
        compiler_params=pltpu.CompilerParams(
            collective_id=0, has_side_effects=True, vmem_limit_bytes=56 << 20
        ),
        cost_estimate=pl.CostEstimate(
            flops=7_500_000_000, bytes_accessed=8 << 20, transcendentals=2 << 20
        ),
        name="infonce",
    )(features[0], weight, pair_ids, dup_ids)
    anywhere = pl.BlockSpec(memory_space=pl.ANY)
    loss, feature_grad, weight_grad = pl.pallas_call(
        deliver,
        out_shape=(
            jax.ShapeDtypeStruct((1, ROWS), F32),
            jax.ShapeDtypeStruct((ROWS, FEAT), BF16),
            jax.ShapeDtypeStruct((16, EMB), F32),
        ),
        in_specs=[anywhere] * 3,
        out_specs=(anywhere,) * 3,
        scratch_shapes=[
            vmem((1, ROWS), F32),
            vmem((ROWS, FEAT), BF16),
            vmem((16, EMB), F32),
            dma((6,)),
            dma((6,)),
        ],
        name="deliver",
    )(loss, feature_grad, weight_grad)
    return loss, feature_grad[None], weight_grad


def solution(mesh):
    return jax.shard_map(
        body,
        mesh=mesh,
        in_specs=(
            P("rep", "loop", None),
            P(("loop", "rep"), None),
            P("rep", "loop"),
            P("rep", "loop"),
        ),
        out_specs=(P("rep", "loop"), P("rep", "loop", None), P(("loop", "rep"), None)),
        check_vma=False,
    )
```

time: 99.1 us -> 84.4 us (0.85)
  Pallas kernels: 93.2 us -> 83.5 us
  local copies, waits for them, and re-layouts: 5.03 us -> 0 us
    pallas_call x1, Pallas kernels: 93.2 us -> 81.1 us  [body(): pl.pallas_call(kernel, out_shape=(jax.ShapeDtypeStruct((1, ROWS), F32), j...]
    unnamed x5 -> x0, local copies, waits for them, and re-layouts: 5.03 us -> none
    pallas_call x0 -> x1, Pallas kernels: none -> 2.46 us  [body(): pl.pallas_call(deliver, out_shape=(jax.ShapeDtypeStruct((1, ROWS), F32),...]
where the time goes in v2:
time: 84.4 us; the launch traced here: 84.2 us
  Pallas kernels  83.5 us (99%)
    pallas_call x1, Pallas kernels, body(): pl.pallas_call(kernel, out_shape=(jax.ShapeDtypeStruct((1, ROWS), F32), j...  81.1 us
    pallas_call x1, Pallas kernels, body(): pl.pallas_call(deliver, out_shape=(jax.ShapeDtypeStruct((1, ROWS), F32),...  2.46 us

profile of v2, /device:TPU:0, one launch (start us, length us, event | category | flops | bytes accessed | tf_op | source)
XLA Modules:
  0.0 84.2 jit_solution(8472874571458331080)
XLA Ops:
  0.6 81.1 %infonce.1 = (f32[1,512]{1,0:T(1,128)}, bf16[512,2048]{1,0:T(8,128)(2,1)}, f32[16,512]{1,0:T(8,128)}) custom-call(bf16[512,2048]{1,0:T(8,128)(2,1)} %bitcast.2, bf16[16,512]{1,0:T(8,128)(2,1)} %weight_ref.1, s32[1,512]{1,0:T(1,128)} %pair_ref.1, s32[1,512]{1,0:T(1,128)} %dup_ref.1), custom_call_target="tpu_custom_call" | custom-call | flops 7500000256 | bytes 8388608 | tf_op jit(solution)/shard_map/infonce/pallas_call | solution.py:657
  81.7 2.5 %deliver.1 = (f32[1,512]{1,0:T(1,128)}, bf16[512,2048]{1,0:T(8,128)(2,1)}, f32[16,512]{1,0:T(8,128)}) custom-call(f32[1,512]{1,0:T(1,128)} %get-tuple-element.9.loss_in, bf16[512,2048]{1,0:T(8,128)(2,1)} %get-tuple-element.10.fgrad_in, f32[16,512]{1,0:T(8,128)} %get-tuple-element.11.wgrad_in), custom_call_target="tpu_custom_call" | custom-call | tf_op jit(solution)/shard_map/deliver/pallas_call | solution.py:746

commit v3 on v2

--- a/solution.py
+++ b/solution.py
@@ -73,6 +73,7 @@
     fgrad_hbm,
     wgrad_ref,
     feat,
+    work,
     featp,
     wpart,
     wfull,
@@ -91,11 +92,10 @@
     pos,
     norms,
     grad,
-    grad_out,
-    grad_in,
-    aux_out,
-    aux_in,
+    loss_out,
+    loss_in,
     pre,
+    home_pre,
     fgrad,
     sib_out,
     sib_in,
@@ -126,6 +126,10 @@
     norm_recv,
     back_send,
     back_recv,
+    loss_send,
+    loss_recv,
+    feat_send,
+    feat_recv,
     rc_send,
     rc_recv,
     rf_send,
@@ -141,7 +145,7 @@
     first = z * other + y * core
     second = y * other + z * core
     stays = core == x_lo
-    slot = core * 4 + z
+    slot = z * 2 + core
 
     def around(value, step):
         return lax.rem(value + step, 4)
@@ -191,7 +195,7 @@
         copy.start()
         started.append(copy)
 
-    lab_swap = remote(label_home, labels.at[other * 4 + z], labx_send.at[0], labx_recv.at[0], partner)
+    lab_swap = remote(label_home, labels.at[z * 2 + other], labx_send.at[0], labx_recv.at[0], partner)
     lab_swap_in = remote(label_home, labels.at[slot], labx_send.at[0], labx_recv.at[0], partner)
 
     @pl.when(jnp.logical_not(stays))
@@ -204,16 +208,21 @@
 
     load.wait()
 
-    def transpose_slab(slab, carry):
-        slab_xlo, slab_z, slab_xhi = lax.div(slab, 8), lax.rem(lax.div(slab, 2), 4), lax.rem(slab, 2)
-        slab_x = slab_xhi * 2 + slab_xlo
-        turned = feat[:, pl.ds(pl.multiple_of(slab * 128, 128), 128)].T
-        for at_y in range(4):
-            zero = pl.multiple_of((at_y * 4 + slab_x) * 16, 16)
-            featp[0, slab_z, pl.ds(zero, 16), :] = turned[at_y * 32 : at_y * 32 + 16]
-            one = pl.multiple_of((slab_z * 4 + slab_x) * 16, 16)
-            featp[1, at_y, pl.ds(one, 16), :] = turned[at_y * 32 + 16 : at_y * 32 + 32]
-        return carry
+    def transpose_half(source, part):
+        rows = pl.ds(part * HALF, HALF)
+
+        def transpose_slab(slab, carry):
+            slab_xlo, slab_z, slab_xhi = lax.div(slab, 8), lax.rem(lax.div(slab, 2), 4), lax.rem(slab, 2)
+            slab_x = slab_xhi * 2 + slab_xlo
+            turned = source[rows, pl.ds(pl.multiple_of(slab * 128, 128), 128)].T
+            for at_y in range(4):
+                zero = pl.multiple_of((slab_z * 4 + slab_x) * 16, 16)
+                featp[0, at_y, pl.ds(zero, 16), rows] = turned[at_y * 32 : at_y * 32 + 16]
+                one = pl.multiple_of((at_y * 4 + slab_x) * 16, 16)
+                featp[1, slab_z, pl.ds(one, 16), rows] = turned[at_y * 32 + 16 : at_y * 32 + 32]
+            return carry
+
+        lax.fori_loop(0, 16, transpose_slab, 0)
 
     def give(source_first, source_second, at):
         copy = remote(
@@ -246,7 +255,19 @@
             started.append(copy)
         give(first, source, piece)
 
-    lax.fori_loop(0, 16, transpose_slab, 0)
+    def follow(chunk):
+        rows = pl.ds(chunk * 128, 128)
+        return remote(feat.at[rows], work.at[rows], feat_send.at[chunk], feat_recv.at[chunk], partner)
+
+    @pl.when(jnp.logical_not(stays))
+    def _():
+        follow(0).start()
+        follow(1).start()
+
+    @pl.when(stays)
+    def _():
+        for part in range(2):
+            transpose_half(feat, part)
 
     @pl.when(jnp.logical_not(stays))
     def _():
@@ -319,24 +340,27 @@
     swaps = [
         remote(
             home_emb.at[pl.ds(part * HALF, HALF)],
-            emb.at[other * 4 + z, pl.ds(part * HALF, HALF)],
+            emb.at[z * 2 + other, pl.ds(part * HALF, HALF)],
             swap_send.at[part],
             swap_recv.at[part],
             partner,
         )
         for part in range(2)
     ]
-    for part in range(2):
+    def project(source, part):
         half_rows = pl.ds(part * HALF, HALF)
-        normed[half_rows, :] = jnp.dot(feat[half_rows, :], wfull[...], preferred_element_type=F32)
+        normed[half_rows, :] = jnp.dot(source[half_rows, :], wfull[...], preferred_element_type=F32)
         for start in range(part * HALF, part * HALF + HALF, 64):
             rows = pl.ds(start, 64)
             projected = normed[rows, :]
             scale = lax.rsqrt(jnp.sum(projected * projected, axis=1, keepdims=True) + norm_eps)
-            unit = projected * scale
-            normed[rows, :] = unit
+            normed[rows, :] = projected * scale
             inverse[rows, :] = jnp.broadcast_to(scale, (64, 128))
-            home_emb[rows, :] = unit.astype(BF16)
+
+    for part in range(2):
+        half_rows = pl.ds(part * HALF, HALF)
+        project(feat, part)
+        home_emb[half_rows, :] = normed[half_rows, :].astype(BF16)
 
         @pl.when(jnp.logical_not(stays))
         def _():
@@ -361,6 +385,8 @@
                 partner,
             ).wait_recv()
             send_own(part)
+        follow(2).start()
+        follow(3).start()
 
     for index in range(7):
         other_slot = lax.rem(slot + 1 + index, 8)
@@ -405,7 +431,7 @@
 
     def next_piece(step, carry):
         which_ring = jnp.where(pick(step, 0) == 0, core, other)
-        at = which_ring * 4 + around(z, pick(step, 1))
+        at = around(z, pick(step, 1)) * 2 + which_ring
         which = pick(step, 2)
         ring(at, which, 1, 0).wait_recv()
 
@@ -426,6 +452,15 @@
                 beside(at, which, count).start()
 
         take(at, which, False)
+        for part in range(2):
+
+            @pl.when(jnp.logical_and(step == (5, 11)[part], jnp.logical_not(stays)))
+            def _():
+                follow(2 * part).wait_recv()
+                follow(2 * part + 1).wait_recv()
+                project(work, part)
+                transpose_half(work, part)
+
         return carry
 
     lax.fori_loop(0, len(ORDER), next_piece, 0)
@@ -442,106 +477,85 @@
         )
         copy.start()
         norm_copies.append(copy)
-    aux_out[...] = jnp.broadcast_to(jnp.log(total_row) - jnp.log(paired_row), (8, ROWS))
+    loss_out[...] = jnp.broadcast_to(jnp.log(total_row) - jnp.log(paired_row), (8, ROWS))
     total = jnp.sum(acc[...] + pos[...], axis=1, keepdims=True)
     acc[...] = jnp.broadcast_to(1.0 / total, (ROWS, 128))
 
     def wait_norm(at):
         remote(norms.at[at], norms.at[at], norm_send.at[0], norm_recv.at[at], sibling).wait_recv()
 
+    loss_back = remote(loss_out, loss_in, loss_send, loss_recv, partner)
+
+    @pl.when(jnp.logical_not(stays))
+    def _():
+        loss_back.start()
+
+    def back(part):
+        rows = pl.ds(part * HALF, HALF)
+        return remote(pre.at[rows], home_pre.at[rows], back_send.at[part], back_recv.at[part], partner)
+
     for part in range(2):
         rows = pl.ds(part * HALF, HALF)
-
-        def add_slots(step, carry):
-            at_z = around(z, jnp.where(step < 2, step, 5 - step))
-            pair = (core * 4 + at_z, other * 4 + at_z)
+        for step in STEPS:
+            pair = around(z, step)
             if part == 0:
-
-                @pl.when(step > 0)
-                def _():
-                    wait_norm(pair[0])
-
-                wait_norm(pair[1])
-            for index, at in enumerate(pair):
-                for lane in range(0, ROWS, 128):
-                    norm = norms[at, 0:1, lane : lane + 128]
+                if step:
+                    wait_norm(pair * 2 + core)
+                wait_norm(pair * 2 + other)
+            buffer = step % 2
+            for index in range(4):
+                for lane in range(0, HALF, 128):
+                    column = (index % 2) * HALF + lane
+                    norm = norms[pair * 2 + index // 2, 0:1, column : column + 128]
                     for start in range(0, HALF, 64):
                         take_rows = pl.ds(part * HALF + start, 64)
-                        value = quot[at * 2 + lane // HALF, take_rows, lane % HALF : lane % HALF + 128]
+                        value = quot[pair * 4 + index, take_rows, lane : lane + 128]
                         weight = jnp.abs(value) * (acc[take_rows, :] + norm) - jnp.where(value < 0.0, 2.0, 0.0)
-                        weights[start : start + 64, index * ROWS + lane : index * ROWS + lane + 128] = weight.astype(BF16)
-            grad[rows, :] += jnp.dot(
-                weights[:, :ROWS], emb[pair[0]], preferred_element_type=F32
-            ) + jnp.dot(weights[:, ROWS:], emb[pair[1]], preferred_element_type=F32)
-            return carry
-
-        grad[rows, :] = jnp.zeros((HALF, EMB), F32)
-        lax.fori_loop(0, 4, add_slots, 0)
+                        weights[buffer, start : start + 64, index * HALF + lane : index * HALF + lane + 128] = (
+                            weight.astype(BF16)
+                        )
+            term = jnp.dot(
+                weights[buffer],
+                emb[pl.ds(pair * 2, 2)].reshape(2 * ROWS, EMB),
+                preferred_element_type=F32,
+            )
+            if step:
+                grad[rows, :] += term
+            else:
+                grad[rows, :] = term
+
+        for start in range(part * HALF, part * HALF + HALF, 64):
+            tile = pl.ds(start, 64)
+            unit = normed[tile, :]
+            whole = scale_logits * grad[tile, :]
+            along = jnp.sum(unit * whole, axis=1, keepdims=True)
+            pre[tile, :] = (inverse[tile, 0:1] * (whole - unit * along)).astype(BF16)
 
         @pl.when(jnp.logical_not(stays))
         def _():
-            unit = emb[slot, rows, :].astype(F32)
-            whole = grad[rows, :]
-            along = jnp.sum(unit * whole, axis=1, keepdims=True)
-            grad_out[rows, :] = (whole - along * unit).astype(BF16)
-            inner = jnp.broadcast_to(along, (HALF, 128)).T[0:1, :]
-            aux_out[1:2, part * HALF : (part + 1) * HALF] = inner
-            remote(
-                grad_out.at[rows], grad_in.at[rows], back_send.at[part], back_recv.at[part], partner
-            ).start()
-
-    @pl.when(jnp.logical_not(stays))
-    def _():
-        remote(aux_out, aux_in, back_send.at[2], back_recv.at[2], partner).start()
-        remote(aux_out, aux_in, back_send.at[2], back_recv.at[2], partner).wait_recv()
-        columns_of = to_column(aux_in[...])
-        loss_ref[...] = aux_in[0:1, :]
-        for part in range(2):
-            rows = pl.ds(part * HALF, HALF)
-            remote(
-                grad_out.at[rows], grad_in.at[rows], back_send.at[part], back_recv.at[part], partner
-            ).wait_recv()
-            along = columns_of[part * HALF : (part + 1) * HALF, 1:2]
-            grad[rows, :] = grad_in[rows, :].astype(F32) + along * home_emb[rows, :].astype(F32)
-
-    @pl.when(stays)
-    def _():
-        loss_ref[...] = aux_out[0:1, :]
-
-    def finish(index, carry):
-        rows = pl.ds(pl.multiple_of(index * 64, 64), 64)
-        unit = normed[rows, :]
-        whole = scale_logits * grad[rows, :]
-        along = jnp.sum(unit * whole, axis=1, keepdims=True)
-        pre[rows, :] = (inverse[rows, 0:1] * (whole - unit * along)).astype(BF16)
-        return carry
-
-    lax.fori_loop(0, 8, finish, 0, unroll=True)
-
-    def term_of(which, at):
-        return jnp.dot(featp[which, at], pre[...], preferred_element_type=F32)
+            back(part).start()
+
+        @pl.when(stays)
+        def _():
+            home_pre[rows, :] = pre[rows, :]
 
     reduce_copies = []
-    for at in range(4):
-        term = term_of(other, at).astype(BF16)
-        for group in range(4):
-            sib_out[group, at] = term[group * 64 : group * 64 + 64]
     for index, offset in enumerate(FAR_FIRST):
         group = around(first, offset)
+        sib_out[group] = jnp.dot(featp[other, group], pre[...], preferred_element_type=F32).astype(BF16)
         copy = remote(sib_out.at[group], sib_in.at[group], rc_send.at[index], rc_recv.at[index], sibling)
         copy.start()
         reduce_copies.append(copy)
     for at in range(4):
-        own_term[at] = term_of(core, at)
+        own_term[at] = jnp.dot(featp[core, at], pre[...], preferred_element_type=F32)
     for index, offset in enumerate(FAR_FIRST):
         group = around(second, offset)
         remote(
             sib_out.at[group], sib_in.at[group], rc_send.at[index], rc_recv.at[index], sibling
         ).wait_recv()
-        rows = pl.ds(pl.multiple_of(group * 64, 64), 64)
         for count, step in enumerate(FAR_FIRST):
-            at = around(first, step)
-            value = own_term[at, rows, :] + sib_in[group, at].astype(F32)
+            rows = pl.ds(pl.multiple_of(around(first, step) * 64, 64), 64)
+            value = own_term[group, rows, :] + sib_in[group, rows, :].astype(F32)
             if step:
                 first_out[index, count] = value.astype(BF16)
                 copy = remote(
@@ -555,17 +569,6 @@
                 reduce_copies.append(copy)
             else:
                 first_sum[index] = value
-
-    def feature_part(index, carry):
-        columns = pl.ds(pl.multiple_of(index * 512, 512), 512)
-        fgrad[:, columns] = lax.dot_general(
-            pre[...], wfull[columns, :], (((1,), (1,)), ((), ())), preferred_element_type=F32
-        ).astype(BF16)
-        return carry
-
-    lax.fori_loop(0, 4, feature_part, 0)
-    store = pltpu.make_async_copy(fgrad, fgrad_hbm, fgrad_sem)
-    store.start()
 
     for index, offset in enumerate(FAR_FIRST):
         whole = first_sum[index]
@@ -593,6 +596,28 @@
                 reduce_copies.append(copy)
         if offset == 0:
             first_sum[index] = whole
+    @pl.when(jnp.logical_not(stays))
+    def _():
+        loss_back.wait_recv()
+        for part in range(2):
+            back(part).wait_recv()
+        loss_ref[...] = loss_in[0:1, :]
+
+    @pl.when(stays)
+    def _():
+        loss_ref[...] = loss_out[0:1, :]
+
+    def feature_part(index, carry):
+        columns = pl.ds(pl.multiple_of(index * 512, 512), 512)
+        fgrad[:, columns] = lax.dot_general(
+            home_pre[...], wfull[columns, :], (((1,), (1,)), ((), ())), preferred_element_type=F32
+        ).astype(BF16)
+        return carry
+
+    lax.fori_loop(0, 4, feature_part, 0)
+    store = pltpu.make_async_copy(fgrad, fgrad_hbm, fgrad_sem)
+    store.start()
+
     value = first_sum[3, pl.ds(pl.multiple_of(x * 16, 16), 16), :]
     for offset in FAR_FIRST:
         for step in (1, 3, 2, 0):
@@ -620,12 +645,11 @@
         lab_swap.wait_send()
         for copy in swaps:
             copy.wait_send()
+        loss_back.wait_send()
         for part in range(2):
-            rows = pl.ds(part * HALF, HALF)
-            remote(
-                grad_out.at[rows], grad_in.at[rows], back_send.at[part], back_recv.at[part], partner
-            ).wait_send()
-        remote(aux_out, aux_in, back_send.at[2], back_recv.at[2], partner).wait_send()
+            back(part).wait_send()
+        for chunk in range(4):
+            follow(chunk).wait_send()
 
     store.wait()
 
@@ -674,6 +698,7 @@
         ),
         scratch_shapes=[
             vmem((ROWS, FEAT), BF16),
+            vmem((ROWS, FEAT), BF16),
             vmem((2, 4, 256, EMB), BF16),
             vmem((2, 4, 4, 4, 16, EMB), BF16),
             vmem((FEAT, EMB), BF16),
@@ -685,21 +710,20 @@
             vmem((8, ROWS), jnp.int32),
             vmem((ROWS, 128), jnp.int32),
             vmem((ROWS, 128), jnp.int32),
-            vmem((HALF, 2 * ROWS), BF16),
+            vmem((2, HALF, 2 * ROWS), BF16),
             vmem((ROWS, HALF), F32),
             vmem((16, ROWS, HALF), F32),
             vmem((ROWS, 128), F32),
             vmem((ROWS, 128), F32),
             vmem((8, 8, ROWS), F32),
             vmem((ROWS, EMB), F32),
-            vmem((ROWS, EMB), BF16),
-            vmem((ROWS, EMB), BF16),
             vmem((8, ROWS), F32),
             vmem((8, ROWS), F32),
             vmem((ROWS, EMB), BF16),
+            vmem((ROWS, EMB), BF16),
             vmem((ROWS, FEAT), BF16),
-            vmem((4, 4, 64, EMB), BF16),
-            vmem((4, 4, 64, EMB), BF16),
+            vmem((4, 256, EMB), BF16),
+            vmem((4, 256, EMB), BF16),
             vmem((4, 256, EMB), F32),
             vmem((4, 3, 64, EMB), BF16),
             vmem((4, 3, 64, EMB), BF16),
@@ -725,8 +749,12 @@
             dma((8, 2)),
             dma((7,)),
             dma((8,)),
-            dma((3,)),
-            dma((3,)),
+            dma((2,)),
+            dma((2,)),
+            dma,
+            dma,
+            dma((4,)),
+            dma((4,)),
             dma((4,)),
             dma((4,)),
             dma((12,)),

time: 84.4 us -> 79.6 us (0.943)
  Pallas kernels: 83.5 us -> 78.8 us
    pallas_call x1, Pallas kernels: 81.1 us -> 76.3 us  [body(): pl.pallas_call(kernel, out_shape=(jax.ShapeDtypeStruct((1, ROWS), F32), j...]
where the time goes in v3:
time: 79.6 us; the launch traced here: 79.4 us
  Pallas kernels  78.8 us (99%)
    pallas_call x1, Pallas kernels, body(): pl.pallas_call(kernel, out_shape=(jax.ShapeDtypeStruct((1, ROWS), F32), j...  76.3 us
    pallas_call x1, Pallas kernels, body(): pl.pallas_call(deliver, out_shape=(jax.ShapeDtypeStruct((1, ROWS), F32),...  2.46 us

profile of v3, /device:TPU:0, one launch (start us, length us, event | category | flops | bytes accessed | tf_op | source)
XLA Modules:
  0.0 79.4 jit_solution(14315917235836645192)
XLA Ops:
  0.6 76.3 %infonce.1 = (f32[1,512]{1,0:T(1,128)}, bf16[512,2048]{1,0:T(8,128)(2,1)}, f32[16,512]{1,0:T(8,128)}) custom-call(bf16[512,2048]{1,0:T(8,128)(2,1)} %bitcast.2, bf16[16,512]{1,0:T(8,128)(2,1)} %weight_ref.1, s32[1,512]{1,0:T(1,128)} %pair_ref.1, s32[1,512]{1,0:T(1,128)} %dup_ref.1), custom_call_target="tpu_custom_call" | custom-call | flops 7500000256 | bytes 8388608 | tf_op jit(solution)/shard_map/infonce/pallas_call | solution.py:681
  77.0 2.5 %deliver.1 = (f32[1,512]{1,0:T(1,128)}, bf16[512,2048]{1,0:T(8,128)(2,1)}, f32[16,512]{1,0:T(8,128)}) custom-call(f32[1,512]{1,0:T(1,128)} %get-tuple-element.9.loss_in, bf16[512,2048]{1,0:T(8,128)(2,1)} %get-tuple-element.10.fgrad_in, f32[16,512]{1,0:T(8,128)} %get-tuple-element.11.wgrad_in), custom_call_target="tpu_custom_call" | custom-call | tf_op jit(solution)/shard_map/deliver/pallas_call | solution.py:774

commit v4 on v3

--- a/solution.py
+++ b/solution.py
@@ -171,9 +171,10 @@
     load.start()
 
     barrier = pltpu.get_barrier_semaphore()
-    everyone = [sibling, partner] + [plane_peer(index) for index in range(1, 16)]
-    for step in (1, 2, 3):
-        everyone += [first_peer(step), z_peer(step, other)]
+    everyone = [plane_peer(index) for index in PLANE]
+    for step in (2, 1, 3):
+        everyone += [z_peer(step, other), first_peer(step)]
+    everyone += [partner, sibling]
     for device in everyone:
         pl.semaphore_signal(barrier, inc=1, device_id=device, device_id_type=MESH)
 
@@ -290,63 +291,62 @@
     row_pairs[...] = jnp.broadcast_to(turned_labels[:, 0:1], (ROWS, 128))
     row_dups[...] = jnp.broadcast_to(turned_labels[:, 1:2], (ROWS, 128))
 
-    for piece in STEPS:
-        at = around(second, 4 - piece)
-        for step in (1, 3, 2):
-            source = around(first, 4 - step)
-            remote(
-                wpart.at[core, source, at],
-                wpart.at[core, source, at],
-                wf_send.at[step - 1, piece],
-                wf_recv.at[step - 1, piece],
-                first_peer(step),
-            ).wait_recv()
-            give(source, at, step * 4 + piece)
-    for piece in STEPS:
-        for step in range(4):
-            block = wpart.at[other, around(second, 4 - step), around(first, 4 - piece)]
+    def place(which, at_first, at_second):
+        at_z = at_first * (1 - which) + at_second * which
+        at_y = at_second * (1 - which) + at_first * which
+        for at_x in range(4):
+            block = (at_x % 2) * 64 + at_z * 16 + (at_x // 2) * 8 + at_y * 2 + which
+            wfull[pl.ds(pl.multiple_of(block * 16, 16), 16), :] = wpart[which, at_first, at_second, at_x]
+
+    for steps in ((1, 3), (2,)):
+        for piece in STEPS:
+            at = around(second, 4 - piece)
+            for step in steps:
+                source = around(first, 4 - step)
+                remote(
+                    wpart.at[core, source, at],
+                    wpart.at[core, source, at],
+                    wf_send.at[step - 1, piece],
+                    wf_recv.at[step - 1, piece],
+                    first_peer(step),
+                ).wait_recv()
+                give(source, at, step * 4 + piece)
+    for at_first in range(4):
+        for at_second in range(4):
+            place(core, at_first, at_second)
+    for step in (0, 1, 3, 2):
+        for piece in STEPS:
+            source = (around(second, 4 - step), around(first, 4 - piece))
+            block = wpart.at[other, source[0], source[1]]
             at = step * 4 + piece
             remote(block, block, wc_send.at[at], wc_recv.at[at], sibling).wait_recv()
-
-    def place_block(index, carry):
-        at_first, at_second, at_x = lax.div(index, 16), lax.rem(lax.div(index, 4), 4), lax.rem(index, 4)
-        base = lax.rem(at_x, 2) * 64 + lax.div(at_x, 2) * 8
-        zero = (base + at_first * 16 + at_second * 2) * 16
-        one = (base + at_second * 16 + at_first * 2 + 1) * 16
-        wfull[pl.ds(pl.multiple_of(zero, 16), 16), :] = wpart[0, at_first, at_second, at_x]
-        wfull[pl.ds(pl.multiple_of(one, 16), 16), :] = wpart[1, at_first, at_second, at_x]
-        return carry
-
-    lax.fori_loop(0, 64, place_block, 0, unroll=8)
-
-    def half(ref, at, which):
-        return ref.at[at, pl.ds(pl.multiple_of(which * HALF, HALF), HALF)]
-
-    def ring(at, which, step, sem):
+            place(other, source[0], source[1])
+
+    def chunk_of(at, chunk):
+        return emb.at[at, pl.ds(pl.multiple_of(chunk * 128, 128), 128)]
+
+    def ring(at, chunk, step, sem):
+        block = chunk_of(at, chunk)
+        return remote(block, block, ring_send.at[sem], emb_recv.at[at, chunk], z_peer(step, core))
+
+    def beside(at, chunk, sem):
+        block = chunk_of(at, chunk)
+        return remote(block, block, sib_send.at[sem], emb_recv.at[at, chunk], sibling)
+
+    def send_own(chunk):
+        ring(slot, chunk, 1, chunk).start()
+        ring(slot, chunk, 3, 4 + chunk).start()
+        beside(slot, chunk, chunk).start()
+
+    def swap(chunk, at):
         return remote(
-            half(emb, at, which), half(emb, at, which), ring_send.at[sem], emb_recv.at[at, which], z_peer(step, core)
-        )
-
-    def beside(at, which, sem):
-        return remote(
-            half(emb, at, which), half(emb, at, which), sib_send.at[sem], emb_recv.at[at, which], sibling
-        )
-
-    def send_own(part):
-        ring(slot, part, 1, part).start()
-        ring(slot, part, 3, 2 + part).start()
-        beside(slot, part, part).start()
-
-    swaps = [
-        remote(
-            home_emb.at[pl.ds(part * HALF, HALF)],
-            emb.at[z * 2 + other, pl.ds(part * HALF, HALF)],
-            swap_send.at[part],
-            swap_recv.at[part],
+            home_emb.at[pl.ds(chunk * 128, 128)],
+            emb.at[at, pl.ds(chunk * 128, 128)],
+            swap_send.at[chunk],
+            swap_recv.at[chunk],
             partner,
         )
-        for part in range(2)
-    ]
+
     def project(source, part):
         half_rows = pl.ds(part * HALF, HALF)
         normed[half_rows, :] = jnp.dot(source[half_rows, :], wfull[...], preferred_element_type=F32)
@@ -364,29 +364,32 @@
 
         @pl.when(jnp.logical_not(stays))
         def _():
-            swaps[part].start()
+            for chunk in (2 * part, 2 * part + 1):
+                swap(chunk, z * 2 + other).start()
 
         @pl.when(stays)
         def _():
             emb[slot, half_rows, :] = home_emb[half_rows, :]
-            send_own(part)
+            for chunk in (2 * part, 2 * part + 1):
+                send_own(chunk)
+
+    def catch_up(part):
+        follow(2 * part).wait_recv()
+        follow(2 * part + 1).wait_recv()
+        project(work, part)
+        transpose_half(work, part)
 
     acc[...] = jnp.zeros((ROWS, 128), F32)
     pos[...] = jnp.zeros((ROWS, 128), F32)
 
     @pl.when(jnp.logical_not(stays))
     def _():
-        for part in range(2):
-            remote(
-                home_emb.at[pl.ds(part * HALF, HALF)],
-                emb.at[slot, pl.ds(part * HALF, HALF)],
-                swap_send.at[part],
-                swap_recv.at[part],
-                partner,
-            ).wait_recv()
-            send_own(part)
+        for chunk in range(4):
+            swap(chunk, slot).wait_recv()
+            send_own(chunk)
         follow(2).start()
         follow(3).start()
+        catch_up(0)
 
     for index in range(7):
         other_slot = lax.rem(slot + 1 + index, 8)
@@ -433,34 +436,27 @@
         which_ring = jnp.where(pick(step, 0) == 0, core, other)
         at = around(z, pick(step, 1)) * 2 + which_ring
         which = pick(step, 2)
-        ring(at, which, 1, 0).wait_recv()
-
-        @pl.when(step == 0)
-        def _():
-            ring(at, which, 1, 4).start()
-            beside(at, which, 2).start()
-
-        @pl.when(step == 3)
-        def _():
-            ring(at, which, 3, 5).start()
-            beside(at, which, 3).start()
-
-        for index, count in ((1, 4), (4, 5), (10, 6), (11, 7)):
-
-            @pl.when(step == index)
+        for sub in range(2):
+            chunk = which * 2 + sub
+            ring(at, chunk, 1, 0).wait_recv()
+
+            @pl.when(step == 0)
             def _():
-                beside(at, which, count).start()
+                ring(at, chunk, 1, 8 + sub).start()
+                beside(at, chunk, 4 + sub).start()
+
+            @pl.when(step == 3)
+            def _():
+                ring(at, chunk, 3, 10 + sub).start()
+                beside(at, chunk, 6 + sub).start()
+
+            for index, count in ((1, 8), (4, 10), (10, 12), (11, 14)):
+
+                @pl.when(step == index)
+                def _():
+                    beside(at, chunk, count + sub).start()
 
         take(at, which, False)
-        for part in range(2):
-
-            @pl.when(jnp.logical_and(step == (5, 11)[part], jnp.logical_not(stays)))
-            def _():
-                follow(2 * part).wait_recv()
-                follow(2 * part + 1).wait_recv()
-                project(work, part)
-                transpose_half(work, part)
-
         return carry
 
     lax.fori_loop(0, len(ORDER), next_piece, 0)
@@ -489,55 +485,52 @@
     @pl.when(jnp.logical_not(stays))
     def _():
         loss_back.start()
+        catch_up(1)
 
     def back(part):
         rows = pl.ds(part * HALF, HALF)
         return remote(pre.at[rows], home_pre.at[rows], back_send.at[part], back_recv.at[part], partner)
 
-    for part in range(2):
-        rows = pl.ds(part * HALF, HALF)
-        for step in STEPS:
-            pair = around(z, step)
-            if part == 0:
-                if step:
-                    wait_norm(pair * 2 + core)
-                wait_norm(pair * 2 + other)
-            buffer = step % 2
-            for index in range(4):
-                for lane in range(0, HALF, 128):
-                    column = (index % 2) * HALF + lane
-                    norm = norms[pair * 2 + index // 2, 0:1, column : column + 128]
-                    for start in range(0, HALF, 64):
-                        take_rows = pl.ds(part * HALF + start, 64)
-                        value = quot[pair * 4 + index, take_rows, lane : lane + 128]
-                        weight = jnp.abs(value) * (acc[take_rows, :] + norm) - jnp.where(value < 0.0, 2.0, 0.0)
-                        weights[buffer, start : start + 64, index * HALF + lane : index * HALF + lane + 128] = (
-                            weight.astype(BF16)
-                        )
-            term = jnp.dot(
-                weights[buffer],
-                emb[pl.ds(pair * 2, 2)].reshape(2 * ROWS, EMB),
-                preferred_element_type=F32,
-            )
-            if step:
-                grad[rows, :] += term
-            else:
-                grad[rows, :] = term
-
-        for start in range(part * HALF, part * HALF + HALF, 64):
-            tile = pl.ds(start, 64)
-            unit = normed[tile, :]
-            whole = scale_logits * grad[tile, :]
-            along = jnp.sum(unit * whole, axis=1, keepdims=True)
-            pre[tile, :] = (inverse[tile, 0:1] * (whole - unit * along)).astype(BF16)
-
-        @pl.when(jnp.logical_not(stays))
-        def _():
+    for step in STEPS:
+        pair = around(z, step)
+        if step:
+            wait_norm(pair * 2 + core)
+        wait_norm(pair * 2 + other)
+        buffer = step % 2
+        for index in range(4):
+            for lane in range(0, HALF, 128):
+                column = (index % 2) * HALF + lane
+                norm = norms[pair * 2 + index // 2, 0:1, column : column + 128]
+                for start in range(0, ROWS, 64):
+                    rows = pl.ds(start, 64)
+                    value = quot[pair * 4 + index, rows, lane : lane + 128]
+                    weight = jnp.abs(value) * (acc[rows, :] + norm) - jnp.where(value < 0.0, 2.0, 0.0)
+                    weights[buffer, start : start + 64, index * HALF + lane : index * HALF + lane + 128] = (
+                        weight.astype(BF16)
+                    )
+        term = jnp.dot(
+            weights[buffer], emb[pl.ds(pair * 2, 2)].reshape(2 * ROWS, EMB), preferred_element_type=F32
+        )
+        if step:
+            grad[...] += term
+        else:
+            grad[...] = term
+
+    for start in range(0, ROWS, 64):
+        rows = pl.ds(start, 64)
+        unit = normed[rows, :]
+        whole = scale_logits * grad[rows, :]
+        along = jnp.sum(unit * whole, axis=1, keepdims=True)
+        pre[rows, :] = (inverse[rows, 0:1] * (whole - unit * along)).astype(BF16)
+
+    @pl.when(jnp.logical_not(stays))
+    def _():
+        for part in range(2):
             back(part).start()
 
-        @pl.when(stays)
-        def _():
-            home_pre[rows, :] = pre[rows, :]
+    @pl.when(stays)
+    def _():
+        home_pre[...] = pre[...]
 
     reduce_copies = []
     for index, offset in enumerate(FAR_FIRST):
@@ -548,8 +541,17 @@
         reduce_copies.append(copy)
     for at in range(4):
         own_term[at] = jnp.dot(featp[core, at], pre[...], preferred_element_type=F32)
-    for index, offset in enumerate(FAR_FIRST):
-        group = around(second, offset)
+    def first_copy(index, count):
+        return remote(
+            first_out.at[index, count],
+            first_in.at[index, count],
+            rf_send.at[index * 3 + count],
+            rf_recv.at[index * 3 + count],
+            first_peer(FAR_FIRST[count]),
+        )
+
+    def send_group(index):
+        group = around(second, FAR_FIRST[index])
         remote(
             sib_out.at[group], sib_in.at[group], rc_send.at[index], rc_recv.at[index], sibling
         ).wait_recv()
@@ -558,28 +560,20 @@
             value = own_term[group, rows, :] + sib_in[group, rows, :].astype(F32)
             if step:
                 first_out[index, count] = value.astype(BF16)
-                copy = remote(
-                    first_out.at[index, count],
-                    first_in.at[index, count],
-                    rf_send.at[index * 3 + count],
-                    rf_recv.at[index * 3 + count],
-                    first_peer(step),
-                )
-                copy.start()
-                reduce_copies.append(copy)
+                first_copy(index, count).start()
             else:
                 first_sum[index] = value
 
+    send_group(0)
+    send_group(1)
     for index, offset in enumerate(FAR_FIRST):
+        for count in range(3):
+            first_copy(index, count).wait_send()
+        if index < 2:
+            send_group(index + 2)
         whole = first_sum[index]
         for count in (1, 2, 0):
-            remote(
-                first_out.at[index, count],
-                first_in.at[index, count],
-                rf_send.at[index * 3 + count],
-                rf_recv.at[index * 3 + count],
-                first_peer(1),
-            ).wait_recv()
+            first_copy(index, count).wait_recv()
             whole = whole + first_in[index, count].astype(F32)
         plane_out[index] = whole.astype(BF16)
         for step in FAR_FIRST:
@@ -635,16 +629,16 @@
 
     for copy in started + lab_copies + norm_copies + reduce_copies:
         copy.wait_send()
-    for index in range(6):
+    for index in range(12):
         ring(slot, 0, 1, index).wait_send()
-    for index in range(8):
+    for index in range(16):
         beside(slot, 0, index).wait_send()
 
     @pl.when(jnp.logical_not(stays))
     def _():
         lab_swap.wait_send()
-        for copy in swaps:
-            copy.wait_send()
+        for chunk in range(4):
+            swap(chunk, z * 2 + other).wait_send()
         loss_back.wait_send()
         for part in range(2):
             back(part).wait_send()
@@ -710,7 +704,7 @@
             vmem((8, ROWS), jnp.int32),
             vmem((ROWS, 128), jnp.int32),
             vmem((ROWS, 128), jnp.int32),
-            vmem((2, HALF, 2 * ROWS), BF16),
+            vmem((2, ROWS, 2 * ROWS), BF16),
             vmem((ROWS, HALF), F32),
             vmem((16, ROWS, HALF), F32),
             vmem((ROWS, 128), F32),
@@ -742,11 +736,11 @@
             dma((8,)),
             dma((1,)),
             dma((1,)),
-            dma((2,)),
-            dma((2,)),
-            dma((6,)),
-            dma((8,)),
-            dma((8, 2)),
+            dma((4,)),
+            dma((4,)),
+            dma((12,)),
+            dma((16,)),
+            dma((8, 4)),
             dma((7,)),
             dma((8,)),
             dma((2,)),

time: 79.6 us -> 75.1 us (0.943)
  Pallas kernels: 78.8 us -> 74.2 us
    pallas_call x1, Pallas kernels: 76.3 us -> 71.8 us  [body(): pl.pallas_call(kernel, out_shape=(jax.ShapeDtypeStruct((1, ROWS), F32), j...]
where the time goes in v4:
time: 75.1 us; the launch traced here: 74.9 us
  Pallas kernels  74.2 us (99%)
    pallas_call x1, Pallas kernels, body(): pl.pallas_call(kernel, out_shape=(jax.ShapeDtypeStruct((1, ROWS), F32), j...  71.8 us
    pallas_call x1, Pallas kernels, body(): pl.pallas_call(deliver, out_shape=(jax.ShapeDtypeStruct((1, ROWS), F32),...  2.46 us

profile of v4, /device:TPU:0, one launch (start us, length us, event | category | flops | bytes accessed | tf_op | source)
XLA Modules:
  0.0 74.9 jit_solution(13661683215752415456)
XLA Ops:
  0.6 71.8 %infonce.1 = (f32[1,512]{1,0:T(1,128)}, bf16[512,2048]{1,0:T(8,128)(2,1)}, f32[16,512]{1,0:T(8,128)}) custom-call(bf16[512,2048]{1,0:T(8,128)(2,1)} %bitcast.2, bf16[16,512]{1,0:T(8,128)(2,1)} %weight_ref.1, s32[1,512]{1,0:T(1,128)} %pair_ref.1, s32[1,512]{1,0:T(1,128)} %dup_ref.1), custom_call_target="tpu_custom_call" | custom-call | flops 7500000256 | bytes 8388608 | tf_op jit(solution)/shard_map/infonce/pallas_call | solution.py:675
  72.4 2.5 %deliver.1 = (f32[1,512]{1,0:T(1,128)}, bf16[512,2048]{1,0:T(8,128)(2,1)}, f32[16,512]{1,0:T(8,128)}) custom-call(f32[1,512]{1,0:T(1,128)} %get-tuple-element.9.loss_in, bf16[512,2048]{1,0:T(8,128)(2,1)} %get-tuple-element.10.fgrad_in, f32[16,512]{1,0:T(8,128)} %get-tuple-element.11.wgrad_in), custom_call_target="tpu_custom_call" | custom-call | tf_op jit(solution)/shard_map/deliver/pallas_call | solution.py:768

commit v5 on v4

--- a/solution.py
+++ b/solution.py
@@ -34,7 +34,7 @@
 )
 STEPS = (0, 1, 3, 2)
 FAR_FIRST = (2, 1, 3, 0)
-PLANE = (10, 6, 14, 9, 11, 2, 8, 5, 7, 13, 15, 1, 3, 4, 12)
+PLANE = (2, 1, 3, 10, 6, 14, 9, 11, 8, 5, 7, 13, 15, 4, 12)
 
 
 def device_at(x, y, z, core):
@@ -66,9 +66,9 @@
 
 def kernel(
     feat_hbm,
-    weight_ref,
-    pair_ref,
-    dup_ref,
+    weight_hbm,
+    pair_hbm,
+    dup_hbm,
     loss_ref,
     fgrad_hbm,
     wgrad_ref,
@@ -105,6 +105,9 @@
     first_sum,
     plane_out,
     plane_in,
+    pair_row,
+    dup_row,
+    small_sem,
     feat_sem,
     fgrad_sem,
     wp_send,
@@ -168,6 +171,13 @@
     partner = device_at(x_hi * 2 + 1 - x_lo, y, z, other)
 
     load = pltpu.make_async_copy(feat_hbm, feat, feat_sem)
+    small_loads = [
+        pltpu.make_async_copy(weight_hbm, wpart.at[core, first, second, x], small_sem.at[0]),
+        pltpu.make_async_copy(pair_hbm, pair_row, small_sem.at[1]),
+        pltpu.make_async_copy(dup_hbm, dup_row, small_sem.at[2]),
+    ]
+    for copy in small_loads:
+        copy.start()
     load.start()
 
     barrier = pltpu.get_barrier_semaphore()
@@ -178,10 +188,11 @@
     for device in everyone:
         pl.semaphore_signal(barrier, inc=1, device_id=device, device_id_type=MESH)
 
-    wpart[core, first, second, x] = weight_ref[...]
     label_home[...] = jnp.zeros((8, ROWS), jnp.int32)
-    label_home[0:1, :] = pair_ref[...]
-    label_home[1:2, :] = dup_ref[...]
+    for copy in small_loads:
+        copy.wait()
+    label_home[0:1, :] = pair_row[...]
+    label_home[1:2, :] = dup_row[...]
     pl.semaphore_wait(barrier, len(everyone))
 
     started = []
@@ -244,7 +255,7 @@
                 remote(
                     block, block, wp_send.at[index - 1], wp_recv.at[index - 1], plane_peer(index)
                 ).wait_recv()
-        for step in (2, 1, 3):
+        for step in (1, 3, 2):
             copy = remote(
                 wpart.at[core, first, source],
                 wpart.at[core, first, source],
@@ -264,11 +275,6 @@
     def _():
         follow(0).start()
         follow(1).start()
-
-    @pl.when(stays)
-    def _():
-        for part in range(2):
-            transpose_half(feat, part)
 
     @pl.when(jnp.logical_not(stays))
     def _():
@@ -382,6 +388,12 @@
     acc[...] = jnp.zeros((ROWS, 128), F32)
     pos[...] = jnp.zeros((ROWS, 128), F32)
 
+    @pl.when(stays)
+    def _():
+        for part in range(2):
+            transpose_half(feat, part)
+
+
     @pl.when(jnp.logical_not(stays))
     def _():
         for chunk in range(4):
@@ -461,8 +473,7 @@
 
     lax.fori_loop(0, len(ORDER), next_piece, 0)
 
-    paired_row = jnp.sum(pos[...].T, axis=0, keepdims=True)
-    total_row = jnp.sum(acc[...].T, axis=0, keepdims=True) + paired_row
+    total_row = jnp.sum((acc[...] + pos[...]).T, axis=0, keepdims=True)
     norms[slot] = jnp.broadcast_to(1.0 / total_row, (8, ROWS))
     norm_copies = []
     for index, (step, which) in enumerate(
@@ -473,6 +484,7 @@
         )
         copy.start()
         norm_copies.append(copy)
+    paired_row = jnp.sum(pos[...].T, axis=0, keepdims=True)
     loss_out[...] = jnp.broadcast_to(jnp.log(total_row) - jnp.log(paired_row), (8, ROWS))
     total = jnp.sum(acc[...] + pos[...], axis=1, keepdims=True)
     acc[...] = jnp.broadcast_to(1.0 / total, (ROWS, 128))
@@ -650,8 +662,8 @@
 
 def deliver(loss_in, fgrad_in, wgrad_in, loss_out, fgrad_out, wgrad_out, loss, fgrad, wgrad, load_sem, store_sem):
     parts = [
-        (fgrad_in.at[pl.ds(at, 128)], fgrad.at[pl.ds(at, 128)], fgrad_out.at[pl.ds(at, 128)])
-        for at in range(0, ROWS, 128)
+        (fgrad_in.at[pl.ds(at, 64)], fgrad.at[pl.ds(at, 64)], fgrad_out.at[pl.ds(at, 64)])
+        for at in range(0, ROWS, 64)
     ]
     parts += [(loss_in, loss, loss_out), (wgrad_in, wgrad, wgrad_out)]
     loads = [
@@ -679,12 +691,7 @@
             jax.ShapeDtypeStruct((ROWS, FEAT), BF16),
             jax.ShapeDtypeStruct((16, EMB), F32),
         ),
-        in_specs=[
-            pl.BlockSpec(memory_space=pl.ANY),
-            pl.BlockSpec(memory_space=vmem),
-            pl.BlockSpec(memory_space=vmem),
-            pl.BlockSpec(memory_space=vmem),
-        ],
+        in_specs=[pl.BlockSpec(memory_space=pl.ANY)] * 4,
         out_specs=(
             pl.BlockSpec(memory_space=vmem),
             pl.BlockSpec(memory_space=pl.ANY),
@@ -724,6 +731,9 @@
             vmem((4, 64, EMB), F32),
             vmem((4, 64, EMB), BF16),
             vmem((15, 16, EMB), BF16),
+            vmem((1, ROWS), jnp.int32),
+            vmem((1, ROWS), jnp.int32),
+            dma((3,)),
             dma,
             dma,
             dma((15,)),
@@ -778,8 +788,8 @@
             vmem((1, ROWS), F32),
             vmem((ROWS, FEAT), BF16),
             vmem((16, EMB), F32),
-            dma((6,)),
-            dma((6,)),
+            dma((10,)),
+            dma((10,)),
         ],
         name="deliver",
     )(loss, feature_grad, weight_grad)

time: 75.1 us -> 73.4 us (0.977)
  Pallas kernels: 74.2 us -> 72.5 us
    pallas_call x1, Pallas kernels: 71.8 us -> 70.1 us  [body(): pl.pallas_call(kernel, out_shape=(jax.ShapeDtypeStruct((1, ROWS), F32), j...]
where the time goes in v5:
time: 73.4 us; the launch traced here: 73.2 us
  Pallas kernels  72.5 us (99%)
    pallas_call x1, Pallas kernels, body(): pl.pallas_call(kernel, out_shape=(jax.ShapeDtypeStruct((1, ROWS), F32), j...  70.1 us
    pallas_call x1, Pallas kernels, body(): pl.pallas_call(deliver, out_shape=(jax.ShapeDtypeStruct((1, ROWS), F32),...  2.43 us

profile of v5, /device:TPU:0, one launch (start us, length us, event | category | flops | bytes accessed | tf_op | source)
XLA Modules:
  0.0 73.2 jit_solution(13085298738801821085)
XLA Ops:
  0.6 70.1 %infonce.1 = (f32[1,512]{1,0:T(1,128)}, bf16[512,2048]{1,0:T(8,128)(2,1)}, f32[16,512]{1,0:T(8,128)}) custom-call(bf16[512,2048]{1,0:T(8,128)(2,1)} %bitcast.2, bf16[16,512]{1,0:T(8,128)(2,1)} %weight_hbm.1, s32[1,512]{1,0:T(1,128)} %pair_hbm.1, s32[1,512]{1,0:T(1,128)} %dup_hbm.1), custom_call_target="tpu_custom_call" | custom-call | flops 7500000256 | bytes 8388608 | tf_op jit(solution)/shard_map/infonce/pallas_call | solution.py:687
  70.8 2.4 %deliver.1 = (f32[1,512]{1,0:T(1,128)}, bf16[512,2048]{1,0:T(8,128)(2,1)}, f32[16,512]{1,0:T(8,128)}) custom-call(f32[1,512]{1,0:T(1,128)} %get-tuple-element.9.loss_in, bf16[512,2048]{1,0:T(8,128)(2,1)} %get-tuple-element.10.fgrad_in, f32[16,512]{1,0:T(8,128)} %get-tuple-element.11.wgrad_in), custom_call_target="tpu_custom_call" | custom-call | tf_op jit(solution)/shard_map/deliver/pallas_call | solution.py:778

commit v6 on v5

--- a/solution.py
+++ b/solution.py
@@ -353,36 +353,37 @@
             partner,
         )
 
-    def project(source, part):
-        half_rows = pl.ds(part * HALF, HALF)
-        normed[half_rows, :] = jnp.dot(source[half_rows, :], wfull[...], preferred_element_type=F32)
-        for start in range(part * HALF, part * HALF + HALF, 64):
-            rows = pl.ds(start, 64)
+    def project(source, start, count):
+        span = pl.ds(start, count)
+        normed[span, :] = jnp.dot(source[span, :], wfull[...], preferred_element_type=F32)
+        for at in range(start, start + count, 64):
+            rows = pl.ds(at, 64)
             projected = normed[rows, :]
             scale = lax.rsqrt(jnp.sum(projected * projected, axis=1, keepdims=True) + norm_eps)
             normed[rows, :] = projected * scale
             inverse[rows, :] = jnp.broadcast_to(scale, (64, 128))
 
-    for part in range(2):
-        half_rows = pl.ds(part * HALF, HALF)
-        project(feat, part)
-        home_emb[half_rows, :] = normed[half_rows, :].astype(BF16)
+    for start, count in ((0, 128), (128, 128), (256, 256)):
+        span = pl.ds(start, count)
+        chunks = range(start // 128, (start + count) // 128)
+        project(feat, start, count)
 
         @pl.when(jnp.logical_not(stays))
         def _():
-            for chunk in (2 * part, 2 * part + 1):
+            home_emb[span, :] = normed[span, :].astype(BF16)
+            for chunk in chunks:
                 swap(chunk, z * 2 + other).start()
 
         @pl.when(stays)
         def _():
-            emb[slot, half_rows, :] = home_emb[half_rows, :]
-            for chunk in (2 * part, 2 * part + 1):
+            emb[slot, span, :] = normed[span, :].astype(BF16)
+            for chunk in chunks:
                 send_own(chunk)
 
     def catch_up(part):
         follow(2 * part).wait_recv()
         follow(2 * part + 1).wait_recv()
-        project(work, part)
+        project(work, part * HALF, HALF)
         transpose_half(work, part)
 
     acc[...] = jnp.zeros((ROWS, 128), F32)
@@ -474,7 +475,7 @@
     lax.fori_loop(0, len(ORDER), next_piece, 0)
 
     total_row = jnp.sum((acc[...] + pos[...]).T, axis=0, keepdims=True)
-    norms[slot] = jnp.broadcast_to(1.0 / total_row, (8, ROWS))
+    norms[slot] = 1.0 / total_row
     norm_copies = []
     for index, (step, which) in enumerate(
         [(0, other)] + [(step, which) for step in (1, 2, 3) for which in (core, other)]
@@ -716,7 +717,7 @@
             vmem((16, ROWS, HALF), F32),
             vmem((ROWS, 128), F32),
             vmem((ROWS, 128), F32),
-            vmem((8, 8, ROWS), F32),
+            vmem((8, 1, ROWS), F32),
             vmem((ROWS, EMB), F32),
             vmem((8, ROWS), F32),
             vmem((8, ROWS), F32),

time: 73.4 us -> 72.8 us (level)
  no operation moved by 1% of the time
where the time goes in v6:
time: 72.8 us; the launch traced here: 72.6 us
  Pallas kernels  72 us (99%)
    pallas_call x1, Pallas kernels, body(): pl.pallas_call(kernel, out_shape=(jax.ShapeDtypeStruct((1, ROWS), F32), j...  69.5 us
    pallas_call x1, Pallas kernels, body(): pl.pallas_call(deliver, out_shape=(jax.ShapeDtypeStruct((1, ROWS), F32),...  2.43 us

profile of v6, /device:TPU:0, one launch (start us, length us, event | category | flops | bytes accessed | tf_op | source)
XLA Modules:
  0.0 72.6 jit_solution(5286370016630440945)
XLA Ops:
  0.6 69.5 %infonce.1 = (f32[1,512]{1,0:T(1,128)}, bf16[512,2048]{1,0:T(8,128)(2,1)}, f32[16,512]{1,0:T(8,128)}) custom-call(bf16[512,2048]{1,0:T(8,128)(2,1)} %bitcast.2, bf16[16,512]{1,0:T(8,128)(2,1)} %weight_hbm.1, s32[1,512]{1,0:T(1,128)} %pair_hbm.1, s32[1,512]{1,0:T(1,128)} %dup_hbm.1), custom_call_target="tpu_custom_call" | custom-call | flops 7500000256 | bytes 8388608 | tf_op jit(solution)/shard_map/infonce/pallas_call | solution.py:688
  70.2 2.4 %deliver.1 = (f32[1,512]{1,0:T(1,128)}, bf16[512,2048]{1,0:T(8,128)(2,1)}, f32[16,512]{1,0:T(8,128)}) custom-call(f32[1,512]{1,0:T(1,128)} %get-tuple-element.9.loss_in, bf16[512,2048]{1,0:T(8,128)(2,1)} %get-tuple-element.10.fgrad_in, f32[16,512]{1,0:T(8,128)} %get-tuple-element.11.wgrad_in), custom_call_target="tpu_custom_call" | custom-call | tf_op jit(solution)/shard_map/deliver/pallas_call | solution.py:779

commit v7 on v6

--- a/solution.py
+++ b/solution.py
@@ -220,6 +220,14 @@
 
     load.wait()
 
+    def follow(chunk):
+        rows = pl.ds(chunk * 128, 128)
+        return remote(feat.at[rows], work.at[rows], feat_send.at[chunk], feat_recv.at[chunk], partner)
+
+    @pl.when(jnp.logical_not(stays))
+    def _():
+        follow(0).start()
+
     def transpose_half(source, part):
         rows = pl.ds(part * HALF, HALF)
 
@@ -267,13 +275,8 @@
             started.append(copy)
         give(first, source, piece)
 
-    def follow(chunk):
-        rows = pl.ds(chunk * 128, 128)
-        return remote(feat.at[rows], work.at[rows], feat_send.at[chunk], feat_recv.at[chunk], partner)
-
     @pl.when(jnp.logical_not(stays))
     def _():
-        follow(0).start()
         follow(1).start()
 
     @pl.when(jnp.logical_not(stays))

time: 72.8 us -> 72.5 us (level)
  no operation moved by 1% of the time
where the time goes in v7:
time: 72.5 us; the launch traced here: 72.3 us
  Pallas kernels  71.7 us (99%)
    pallas_call x1, Pallas kernels, body(): pl.pallas_call(kernel, out_shape=(jax.ShapeDtypeStruct((1, ROWS), F32), j...  69.3 us
    pallas_call x1, Pallas kernels, body(): pl.pallas_call(deliver, out_shape=(jax.ShapeDtypeStruct((1, ROWS), F32),...  2.43 us

profile of v7, /device:TPU:0, one launch (start us, length us, event | category | flops | bytes accessed | tf_op | source)
XLA Modules:
  0.0 72.3 jit_solution(6501935603900036275)
XLA Ops:
  0.6 69.3 %infonce.1 = (f32[1,512]{1,0:T(1,128)}, bf16[512,2048]{1,0:T(8,128)(2,1)}, f32[16,512]{1,0:T(8,128)}) custom-call(bf16[512,2048]{1,0:T(8,128)(2,1)} %bitcast.2, bf16[16,512]{1,0:T(8,128)(2,1)} %weight_hbm.1, s32[1,512]{1,0:T(1,128)} %pair_hbm.1, s32[1,512]{1,0:T(1,128)} %dup_hbm.1), custom_call_target="tpu_custom_call" | custom-call | flops 7500000256 | bytes 8388608 | tf_op jit(solution)/shard_map/infonce/pallas_call | solution.py:691
  69.9 2.4 %deliver.1 = (f32[1,512]{1,0:T(1,128)}, bf16[512,2048]{1,0:T(8,128)(2,1)}, f32[16,512]{1,0:T(8,128)}) custom-call(f32[1,512]{1,0:T(1,128)} %get-tuple-element.9.loss_in, bf16[512,2048]{1,0:T(8,128)(2,1)} %get-tuple-element.10.fgrad_in, f32[16,512]{1,0:T(8,128)} %get-tuple-element.11.wgrad_in), custom_call_target="tpu_custom_call" | custom-call | tf_op jit(solution)/shard_map/deliver/pallas_call | solution.py:782

commit v8 on v7

--- a/solution.py
+++ b/solution.py
@@ -544,10 +544,6 @@
         for part in range(2):
             back(part).start()
 
-    @pl.when(stays)
-    def _():
-        home_pre[...] = pre[...]
-
     reduce_copies = []
     for index, offset in enumerate(FAR_FIRST):
         group = around(first, offset)
@@ -616,6 +612,7 @@
     @pl.when(stays)
     def _():
         loss_ref[...] = loss_out[0:1, :]
+        home_pre[...] = pre[...]
 
     def feature_part(index, carry):
         columns = pl.ds(pl.multiple_of(index * 512, 512), 512)

time: 72.5 us -> 72.5 us (level)
  no operation moved by 1% of the time
where the time goes in v8:
time: 72.5 us; the launch traced here: 72.4 us
  Pallas kernels  71.7 us (99%)
    pallas_call x1, Pallas kernels, body(): pl.pallas_call(kernel, out_shape=(jax.ShapeDtypeStruct((1, ROWS), F32), j...  69.3 us
    pallas_call x1, Pallas kernels, body(): pl.pallas_call(deliver, out_shape=(jax.ShapeDtypeStruct((1, ROWS), F32),...  2.43 us

profile of v8, /device:TPU:0, one launch (start us, length us, event | category | flops | bytes accessed | tf_op | source)
XLA Modules:
  0.0 72.4 jit_solution(14786457351829032503)
XLA Ops:
  0.6 69.3 %infonce.1 = (f32[1,512]{1,0:T(1,128)}, bf16[512,2048]{1,0:T(8,128)(2,1)}, f32[16,512]{1,0:T(8,128)}) custom-call(bf16[512,2048]{1,0:T(8,128)(2,1)} %bitcast.2, bf16[16,512]{1,0:T(8,128)(2,1)} %weight_hbm.1, s32[1,512]{1,0:T(1,128)} %pair_hbm.1, s32[1,512]{1,0:T(1,128)} %dup_hbm.1), custom_call_target="tpu_custom_call" | custom-call | flops 7500000256 | bytes 8388608 | tf_op jit(solution)/shard_map/infonce/pallas_call | solution.py:688
  69.9 2.4 %deliver.1 = (f32[1,512]{1,0:T(1,128)}, bf16[512,2048]{1,0:T(8,128)(2,1)}, f32[16,512]{1,0:T(8,128)}) custom-call(f32[1,512]{1,0:T(1,128)} %get-tuple-element.9.loss_in, bf16[512,2048]{1,0:T(8,128)(2,1)} %get-tuple-element.10.fgrad_in, f32[16,512]{1,0:T(8,128)} %get-tuple-element.11.wgrad_in), custom_call_target="tpu_custom_call" | custom-call | tf_op jit(solution)/shard_map/deliver/pallas_call | solution.py:779
